TPU v7x, 32 devices: a whole 2x2x4 slice. The times are simulated.
32 devices in a mesh: img: 8 (over z, x), seq: 4 (over y, core).
Axes of the slice: x: 2, y: 2, z: 4, core: 2. Of those that a mesh axis runs over, the one named last changes fastest.
Arguments:
- tokens: bfloat16 [16, 1024, 1152], P('img', 'seq'), may hold values from -6 to 6
- time_embed: bfloat16 [16, 4, 1152], P('img'), may hold values from -6 to 6
- image_lengths: int32 [16, 4], P('img'), may hold values from 0 to 1024, as said below
- grid_turns: int32 [16, 4], P('img'), may hold values from 0 to 7
- ln1_gain: float32 [1152], replicated, may hold values from 0.5 to 1.5
- w_qkv: bfloat16 [1152, 3456], replicated, may hold values from -0.1875 to 0.1875
- w_time_q: bfloat16 [1152, 1152], replicated, may hold values from -0.1875 to 0.1875
- time_value_weight: bfloat16 [1152, 1152], replicated, may hold values from -0.0234375 to 0.0234375
- rel_rows: float32 [16, 63], replicated, may hold values from -3 to 3
- rel_cols: float32 [16, 63], replicated, may hold values from -3 to 3
- output_projection_weight: bfloat16 [1152, 1152], replicated, may hold values from -1.5 to 1.5
- ln2_gain: float32 [1152], replicated, may hold values from 0.5 to 1.5
- w_up: bfloat16 [1152, 4608], replicated, may hold values from -0.1875 to 0.1875
- w_down: bfloat16 [4608, 1152], replicated, may hold values from -0.09375 to 0.09375
- out_grad: bfloat16 [16, 1024, 1152], P('img', 'seq'), may hold values from -6 to 6
Outputs:
- output: bfloat16 [16, 1024, 1152], P('img', 'seq')
- input_grad: bfloat16 [16, 1024, 1152], P('img', 'seq')
- ln1_gain_grad: float32 [1152], P('img')
- w_qkv_grad: float32 [1152, 3456], P('img')
- w_time_q_grad: float32 [1152, 1152], P('img')
- w_time_v_grad: float32 [1152, 1152], P('img')
- rel_rows_grad: float32 [16, 63], replicated
- rel_cols_grad: float32 [16, 63], replicated
- w_proj_grad: float32 [1152, 1152], P('img')
- ln2_gain_grad: float32 [1152], P('img')
- w_up_grad: float32 [1152, 4608], P('img')
- w_down_grad: float32 [4608, 1152], P('img')
- rms_values: float32 [3], replicated
Inputs may be any that keep to these rules, and one draw needn't show every extreme that they name: `image_lengths`: A slot holds one image of 1024 tokens, or one to four images of 256 tokens, or nothing; images come first, the rest of its 1024 tokens is padding. Every group of 2 slots along img has a slot with a 1024-token image, and one group has no empty slot. `grid_turns`: bit 0 flips the grid's rows, bit 1 its columns, bit 2 swaps rows and columns.
All inputs are finite; a program needn't handle non-finite values.
Results may differ from a plain program's by a relative error of at most 0.022.
Values may be sent and summed in bfloat16 or wider, within the bound.
No kernel may reach another device: no remote copies, remote signals or barrier semaphores. Data moves between devices by JAX's collectives and lax.ppermute only.
A program may use at most 384 MiB of HBM per device.

v0:
```python
import jax
import jax.numpy as jnp
from jax import lax
from jax.sharding import PartitionSpec as P

SIDE = 32


eps_norm = 1e-06
peak_value = lax.Precision.HIGHEST


def shifted(block, axis, distance):
    devices = range(lax.axis_size(axis))
    route = [((i - distance) % len(devices), i) for i in devices]
    return lax.ppermute(block, axis, route)


def layout(lengths, turn_codes, positions, grid_side):
    image_end = jnp.cumsum(lengths, axis=1, dtype=jnp.int32)
    image_start = image_end - lengths
    token_at = positions[None, :]
    segment = jnp.sum(
        (token_at[:, :, None] >= image_end[:, None, :]).astype(jnp.int32), axis=2, dtype=jnp.int32
    )
    is_valid = token_at < image_end[:, 3:4]
    picked = jnp.minimum(segment, 3)
    onehot = (picked[:, :, None] == jnp.arange(4, dtype=jnp.int32)[None, None, :]).astype(jnp.int32)
    begin_at = jnp.sum(onehot * image_start[:, None, :], axis=2, dtype=jnp.int32)
    image_len = jnp.sum(onehot * lengths[:, None, :], axis=2, dtype=jnp.int32)
    turned = jnp.sum(onehot * turn_codes[:, None, :], axis=2, dtype=jnp.int32)
    grid_width = jnp.where(image_len == grid_side * grid_side, grid_side, grid_side // 2).astype(
        jnp.int32
    )
    offset = token_at - begin_at
    row_raw = offset // grid_width
    col_raw = offset % grid_width
    row_flip = jnp.where(turned % 2 == 1, grid_width - 1 - row_raw, row_raw)
    col_flip = jnp.where(turned // 2 % 2 == 1, grid_width - 1 - col_raw, col_raw)
    row_pos = jnp.where(turned >= 4, col_flip, row_flip)
    col_pos = jnp.where(turned >= 4, row_flip, col_flip)
    row_pos = jnp.where(is_valid, row_pos, 0)
    col_pos = jnp.where(is_valid, col_pos, 0)
    return (segment, is_valid, row_pos, col_pos, onehot)


def layer_norm(inputs, gain_vec):
    centre = inputs - jnp.mean(inputs, axis=-1, keepdims=True)
    spread = jnp.mean(centre * centre, axis=-1, keepdims=True)
    return centre * lax.rsqrt(spread + eps_norm) * gain_vec


def gelu_exact(inputs):
    return jax.nn.gelu(inputs, approximate=False)


def one_hot(index, count):
    return (index[..., None] == jnp.arange(count, dtype=jnp.int32)).astype(jnp.bfloat16)


def toeplitz(table, grid_side):
    offsets = jnp.arange(grid_side, dtype=jnp.int32)
    return table[:, offsets[:, None] - offsets[None, :] + grid_side - 1]


def diagonals(grid_side):
    offsets = jnp.arange(grid_side, dtype=jnp.int32)
    spread_idx = offsets[:, None] - offsets[None, :] + grid_side - 1
    return (spread_idx[:, :, None] == jnp.arange(2 * grid_side - 1, dtype=jnp.int32)).astype(
        jnp.float32
    )


def key_features(key_block, lengths, turn_codes, source, head_count, grid_side):
    slot_count, span_len, model_dim = key_block.shape
    positions = source * span_len + jnp.arange(span_len, dtype=jnp.int32)
    segment, is_valid, row_pos, col_pos, onehot = layout(lengths, turn_codes, positions, grid_side)
    hot_shape = (slot_count, span_len, head_count, grid_side)
    row_hot = jnp.broadcast_to(one_hot(row_pos, grid_side)[:, :, None, :], hot_shape)
    col_hot = jnp.broadcast_to(one_hot(col_pos, grid_side)[:, :, None, :], hot_shape)
    split_keys = key_block.reshape(slot_count, span_len, head_count, model_dim // head_count)
    return (jnp.concatenate([split_keys, row_hot, col_hot], axis=3), segment)


def masked_scores(query_aug, key_aug, query_seg, key_seg):
    products = jnp.einsum("sqhf,skhf->shqk", query_aug, key_aug, preferred_element_type=jnp.float32)
    same_image = query_seg[:, None, :, None] == key_seg[:, None, None, :]
    return jnp.where(same_image, products, -1e30)


def per_device(
    tokens,
    time_embed,
    image_lengths,
    grid_turns,
    ln1_gain,
    w_qkv,
    w_time_q,
    time_value_weight,
    rel_rows,
    rel_cols,
    output_projection_weight,
    ln2_gain,
    w_up,
    w_down,
    out_grad,
):
    slot_count, span_len, model_dim = tokens.shape
    head_count = rel_rows.shape[0]
    head_dim = model_dim // head_count
    q_scale = head_dim ** (-0.5)
    grid_side = SIDE
    row_total = slot_count * span_len
    seq_count = lax.axis_size("seq")
    local_index = lax.axis_index("seq")
    positions = local_index * span_len + jnp.arange(span_len, dtype=jnp.int32)
    query_seg, is_valid, row_pos, col_pos, onehot = layout(
        image_lengths, grid_turns, positions, grid_side
    )
    image_hot = onehot.astype(jnp.float32)
    valid_mask = is_valid.astype(jnp.float32).reshape(row_total, 1)
    x_float = tokens.astype(jnp.float32).reshape(row_total, model_dim)
    attn_in = layer_norm(x_float, ln1_gain).astype(jnp.bfloat16)
    qkv_full = jnp.dot(attn_in, w_qkv, preferred_element_type=jnp.float32).reshape(
        slot_count, span_len, 3 * model_dim
    )
    time_q = jnp.einsum("sjd,df->sjf", time_embed, w_time_q, preferred_element_type=jnp.float32)
    time_v = jnp.einsum(
        "sjd,df->sjf", time_embed, time_value_weight, preferred_element_type=jnp.float32
    )
    token_tq = jnp.einsum("snj,sjf->snf", image_hot, time_q, precision=peak_value)
    token_tv = jnp.einsum("snj,sjf->snf", image_hot, time_v, precision=peak_value)
    queries = ((qkv_full[..., :model_dim] + token_tq) * q_scale).astype(jnp.bfloat16)
    keys = qkv_full[..., model_dim : 2 * model_dim].astype(jnp.bfloat16)
    values = (qkv_full[..., 2 * model_dim :] + token_tv).astype(jnp.bfloat16)
    row_table = toeplitz(rel_rows.astype(jnp.bfloat16), grid_side)
    col_table = toeplitz(rel_cols.astype(jnp.bfloat16), grid_side)
    row_hot_q = one_hot(row_pos, grid_side)
    col_hot_q = one_hot(col_pos, grid_side)
    row_bias = jnp.einsum(
        "scr,hrt->scht", row_hot_q, row_table, preferred_element_type=jnp.float32
    ).astype(jnp.bfloat16)
    col_bias = jnp.einsum(
        "scr,hrt->scht", col_hot_q, col_table, preferred_element_type=jnp.float32
    ).astype(jnp.bfloat16)
    query_aug = jnp.concatenate(
        [queries.reshape(slot_count, span_len, head_count, head_dim), row_bias, col_bias], axis=3
    )
    row_max = jnp.full((slot_count, head_count, span_len), -1e30, jnp.float32)
    row_sum = jnp.zeros((slot_count, head_count, span_len), jnp.float32)
    weighted = jnp.zeros((slot_count, span_len, head_count, head_dim), jnp.float32)
    key_block, value_block = (keys, values)
    for rotation in range(seq_count):
        source = (local_index - rotation) % seq_count
        key_aug, key_seg = key_features(
            key_block, image_lengths, grid_turns, source, head_count, grid_side
        )
        score_matrix = masked_scores(query_aug, key_aug, query_seg, key_seg)
        new_max = jnp.maximum(row_max, jnp.max(score_matrix, axis=3))
        rescale = jnp.exp(row_max - new_max)
        exps = jnp.exp(score_matrix - new_max[..., None])
        row_sum = row_sum * rescale + jnp.sum(exps, axis=3)
        value_heads = value_block.reshape(slot_count, span_len, head_count, head_dim)
        weighted = weighted * jnp.transpose(rescale, (0, 2, 1))[..., None] + jnp.einsum(
            "shqk,skhe->sqhe",
            exps.astype(jnp.bfloat16),
            value_heads,
            preferred_element_type=jnp.float32,
        )
        row_max = new_max
        if rotation + 1 < seq_count:
            key_block, value_block = shifted((key_block, value_block), "seq", 1)
    attn_float = weighted / jnp.transpose(row_sum, (0, 2, 1))[..., None]
    log_norm = row_max + jnp.log(row_sum)
    attention_result = attn_float.reshape(row_total, model_dim).astype(jnp.bfloat16)
    first_branch = jnp.dot(
        attention_result, output_projection_weight, preferred_element_type=jnp.float32
    )
    hidden_one = x_float + first_branch
    mlp_in = layer_norm(hidden_one, ln2_gain).astype(jnp.bfloat16)
    up_proj = jnp.dot(mlp_in, w_up, preferred_element_type=jnp.float32)
    gelu_out = gelu_exact(up_proj).astype(jnp.bfloat16)
    branch_two = jnp.dot(gelu_out, w_down, preferred_element_type=jnp.float32)
    hidden_two = hidden_one + branch_two
    output = (hidden_two * valid_mask).astype(jnp.bfloat16).reshape(slot_count, span_len, model_dim)
    stats = jnp.stack(
        [
            jnp.sum(valid_mask * hidden_two * hidden_two),
            jnp.sum(valid_mask * first_branch * first_branch),
            jnp.sum(valid_mask * branch_two * branch_two),
            jnp.sum(valid_mask),
        ]
    )
    grad_two = out_grad.astype(jnp.float32).reshape(row_total, model_dim) * valid_mask
    grad_branch = grad_two.astype(jnp.bfloat16)
    w_down_grad = jnp.einsum("nf,nd->fd", gelu_out, grad_branch, preferred_element_type=jnp.float32)
    grad_gelu = jnp.einsum("nd,fd->nf", grad_branch, w_down, preferred_element_type=jnp.float32)
    unused_gelu, gelu_pull = jax.vjp(gelu_exact, up_proj)
    grad_up = gelu_pull(grad_gelu)[0].astype(jnp.bfloat16)
    w_up_grad = jnp.einsum("nd,nf->df", mlp_in, grad_up, preferred_element_type=jnp.float32)
    grad_mlp_in = jnp.einsum("nf,df->nd", grad_up, w_up, preferred_element_type=jnp.float32)
    unused_norm, norm_pull = jax.vjp(layer_norm, hidden_one, ln2_gain)
    grad_back_two, ln2_gain_grad = norm_pull(grad_mlp_in)
    grad_one = grad_two + grad_back_two
    grad_b1 = grad_one.astype(jnp.bfloat16)
    w_proj_grad = jnp.einsum(
        "nd,ne->de", attention_result, grad_b1, preferred_element_type=jnp.float32
    )
    grad_attn = (
        jnp.einsum(
            "ne,de->nd", grad_b1, output_projection_weight, preferred_element_type=jnp.float32
        )
        .astype(jnp.bfloat16)
        .reshape(slot_count, span_len, head_count, head_dim)
    )
    row_delta = jnp.transpose(
        jnp.sum(grad_attn.astype(jnp.float32) * attn_float, axis=3), (0, 2, 1)
    )
    grad_query = jnp.zeros(
        (slot_count, span_len, head_count, head_dim + 2 * grid_side), jnp.float32
    )
    grad_keys = jnp.zeros((slot_count, span_len, model_dim), jnp.float32)
    grad_values = jnp.zeros((slot_count, span_len, model_dim), jnp.float32)
    key_block, value_block = (keys, values)
    for rotation in range(seq_count):
        source = (local_index - rotation) % seq_count
        key_aug, key_seg = key_features(
            key_block, image_lengths, grid_turns, source, head_count, grid_side
        )
        score_matrix = masked_scores(query_aug, key_aug, query_seg, key_seg)
        probs = jnp.exp(score_matrix - log_norm[..., None])
        value_heads = value_block.reshape(slot_count, span_len, head_count, head_dim)
        grad_probs = jnp.einsum(
            "sqhe,skhe->shqk", grad_attn, value_heads, preferred_element_type=jnp.float32
        )
        grad_scores = (probs * (grad_probs - row_delta[..., None])).astype(jnp.bfloat16)
        grad_query = grad_query + jnp.einsum(
            "shqk,skhf->sqhf", grad_scores, key_aug, preferred_element_type=jnp.float32
        )
        part_keys = jnp.einsum(
            "shqk,sqhe->skhe",
            grad_scores,
            query_aug[..., :head_dim],
            preferred_element_type=jnp.float32,
        ).reshape(slot_count, span_len, model_dim)
        part_values = jnp.einsum(
            "shqk,sqhe->skhe",
            probs.astype(jnp.bfloat16),
            grad_attn,
            preferred_element_type=jnp.float32,
        ).reshape(slot_count, span_len, model_dim)
        grad_keys, grad_values = (
            shifted((grad_keys + part_keys).astype(jnp.bfloat16), "seq", 1).astype(jnp.float32),
            shifted((grad_values + part_values).astype(jnp.bfloat16), "seq", 1).astype(jnp.float32),
        )
        if rotation + 1 < seq_count:
            key_block, value_block = shifted((key_block, value_block), "seq", 1)
    grad_z = (
        (grad_query[..., :head_dim] * q_scale)
        .astype(jnp.bfloat16)
        .reshape(slot_count, span_len, model_dim)
    )
    grad_row_bias = grad_query[..., head_dim : head_dim + grid_side]
    grad_col_bias = grad_query[..., head_dim + grid_side :]
    diag_hot = diagonals(grid_side)
    row_toe = jnp.einsum(
        "scr,scht->hrt", row_hot_q.astype(jnp.float32), grad_row_bias, precision=peak_value
    )
    col_toe = jnp.einsum(
        "scr,scht->hrt", col_hot_q.astype(jnp.float32), grad_col_bias, precision=peak_value
    )
    rel_rows_grad = jnp.einsum("hrt,rtd->hd", row_toe, diag_hot, precision=peak_value)
    rel_cols_grad = jnp.einsum("hrt,rtd->hd", col_toe, diag_hot, precision=peak_value)
    grad_k = grad_keys.astype(jnp.bfloat16)
    grad_v = grad_values.astype(jnp.bfloat16)
    time_float = time_embed.astype(jnp.float32)
    image_grad_q = jnp.einsum(
        "snj,snd->sjd", image_hot, grad_z.astype(jnp.float32), precision=peak_value
    )
    image_grad_v = jnp.einsum(
        "snj,snd->sjd", image_hot, grad_v.astype(jnp.float32), precision=peak_value
    )
    w_time_q_grad = jnp.einsum("sjd,sjf->df", time_float, image_grad_q, precision=peak_value)
    w_time_v_grad = jnp.einsum("sjd,sjf->df", time_float, image_grad_v, precision=peak_value)
    grad_qkv = jnp.concatenate([grad_z, grad_k, grad_v], axis=2).reshape(row_total, 3 * model_dim)
    w_qkv_grad = jnp.einsum("nd,nf->df", attn_in, grad_qkv, preferred_element_type=jnp.float32)
    grad_attn_in = jnp.einsum("nf,df->nd", grad_qkv, w_qkv, preferred_element_type=jnp.float32)
    unused_first, first_pull = jax.vjp(layer_norm, x_float, ln1_gain)
    grad_back_one, ln1_gain_grad = first_pull(grad_attn_in)
    input_grad = (
        (grad_one + grad_back_one).astype(jnp.bfloat16).reshape(slot_count, span_len, model_dim)
    )
    (
        ln1_gain_grad,
        w_qkv_grad,
        w_time_q_grad,
        w_time_v_grad,
        w_proj_grad,
        ln2_gain_grad,
        w_up_grad,
        w_down_grad,
    ) = (
        lax.psum_scatter(
            ln1_gain_grad.astype(jnp.bfloat16), "img", scatter_dimension=0, tiled=True
        ).astype(jnp.float32),
        lax.psum_scatter(
            w_qkv_grad.astype(jnp.bfloat16), "img", scatter_dimension=0, tiled=True
        ).astype(jnp.float32),
        lax.psum_scatter(
            w_time_q_grad.astype(jnp.bfloat16), "img", scatter_dimension=0, tiled=True
        ).astype(jnp.float32),
        lax.psum_scatter(
            w_time_v_grad.astype(jnp.bfloat16), "img", scatter_dimension=0, tiled=True
        ).astype(jnp.float32),
        lax.psum_scatter(
            w_proj_grad.astype(jnp.bfloat16), "img", scatter_dimension=0, tiled=True
        ).astype(jnp.float32),
        lax.psum_scatter(
            ln2_gain_grad.astype(jnp.bfloat16), "img", scatter_dimension=0, tiled=True
        ).astype(jnp.float32),
        lax.psum_scatter(
            w_up_grad.astype(jnp.bfloat16), "img", scatter_dimension=0, tiled=True
        ).astype(jnp.float32),
        lax.psum_scatter(
            w_down_grad.astype(jnp.bfloat16), "img", scatter_dimension=0, tiled=True
        ).astype(jnp.float32),
    )
    (
        ln1_gain_grad,
        w_qkv_grad,
        w_time_q_grad,
        w_time_v_grad,
        w_proj_grad,
        ln2_gain_grad,
        w_up_grad,
        w_down_grad,
    ) = (
        lax.psum(ln1_gain_grad.astype(jnp.bfloat16), "seq").astype(jnp.float32),
        lax.psum(w_qkv_grad.astype(jnp.bfloat16), "seq").astype(jnp.float32),
        lax.psum(w_time_q_grad.astype(jnp.bfloat16), "seq").astype(jnp.float32),
        lax.psum(w_time_v_grad.astype(jnp.bfloat16), "seq").astype(jnp.float32),
        lax.psum(w_proj_grad.astype(jnp.bfloat16), "seq").astype(jnp.float32),
        lax.psum(ln2_gain_grad.astype(jnp.bfloat16), "seq").astype(jnp.float32),
        lax.psum(w_up_grad.astype(jnp.bfloat16), "seq").astype(jnp.float32),
        lax.psum(w_down_grad.astype(jnp.bfloat16), "seq").astype(jnp.float32),
    )
    rel_rows_grad, rel_cols_grad, stats = lax.psum(
        (rel_rows_grad, rel_cols_grad, stats), ("img", "seq")
    )
    rms_values = jnp.sqrt(stats[:3] / (stats[3] * model_dim))
    return (
        output,
        input_grad,
        ln1_gain_grad,
        w_qkv_grad,
        w_time_q_grad,
        w_time_v_grad,
        rel_rows_grad,
        rel_cols_grad,
        w_proj_grad,
        ln2_gain_grad,
        w_up_grad,
        w_down_grad,
        rms_values,
    )


def solution(mesh):
    return jax.shard_map(
        per_device,
        mesh=mesh,
        in_specs=(
            P("img", "seq", None),
            P("img", None, None),
            P("img", None),
            P("img", None),
            P(),
            P(),
            P(),
            P(),
            P(),
            P(),
            P(),
            P(),
            P(),
            P(),
            P("img", "seq", None),
        ),
        out_specs=(
            P("img", "seq", None),
            P("img", "seq", None),
            P("img"),
            P("img", None),
            P("img", None),
            P("img", None),
            P(),
            P(),
            P("img", None),
            P("img"),
            P("img", None),
            P("img", None),
            P(),
        ),
        check_vma=False,
    )
```

profile of v0, /device:TPU:0, one launch (start us, length us, event | category | flops | bytes accessed | tf_op | source)
XLA Modules:
  0.0 1165.0 jit_solution(7323225410281309872)
XLA Ops:
  11.8 7.8 fusion.6
  26.7 4.8 fusion.66
  42.4 4.8 fusion.65
  65.3 4.3 select_reduce_fusion.3
  75.8 4.1 collective-permute-done.2
  81.1 7.0 select_reduce_fusion.2
  95.2 7.2 select_reduce_fusion.1
  108.1 7.4 select_reduce_fusion
  117.3 5.7 fusion.16
  139.2 9.4 fusion.195
  154.3 6.4 fusion.188
  160.7 31.3 %add_convert_fusion = (bf16[512,4608]{1,0:T(8,128)(2,1)}, f32[512,4608]{1,0:T(8,128)}) fusion(f32[512,4608]{1,0:T(8,128)S(1)} %fusion.188, bf16[512,1152]{1,0:T(8,128)(2,1)S(1)} %copy-done.70, bf16[4608,1152]{1,0:T(8,128)(2,1)} %param.28), kind=kOutput, calls=%fused_computation.7 | convolution fusion | flops 5605687296 | bytes 35389440 | tf_op jit(solution)/shard_map/nd,fd->nf/dot_general | solution.py:197
  192.0 10.7 multiply_convert_fusion
  202.7 10.3 fusion.196
  213.0 12.7 %fusion.71 = (f32[]{:T(128)}, f32[]{:T(128)}, f32[512]{0:T(512)S(1)}, bf16[1152]{0:T(1024)(128)(2,1)S(1)}, f32[]{:T(128)}, /*index=5*/bf16[512,1152]{1,0:T(8,128)(2,1)}) fusion(f32[512]{0:T(512)S(1)} %bitcast.368, f32[512,1152]{1,0:T(8,128)S(1)} %copy-done.12, f32[512,1152]{1,0:T(8,128)S(1)} %fusion.196, f32[1152]{0:T(1024)S(1)} %copy-done.102, ...), kind=kOutput, calls=%fused_computation.109 | convolution fusion | flops 5446433280 | bytes 23608076 | tf_op jit(solution)/shard_map/dot_general | solution.py:183
  231.9 5.7 reshape.1310
  242.6 6.3 fusion.96
  248.9 6.4 multiply_convert_fusion.4
  255.4 3.9 multiply_convert_fusion.1
  259.4 3.9 multiply_convert_fusion.2
  266.4 3.8 multiply_convert_fusion.3
  272.8 5.3 fusion.105
  284.1 3.8 fusion.103
  289.8 4.0 add_bitcast_fusion
  300.3 4.1 fusion.23
  304.4 5.2 copy.331
  309.7 6.5 fusion.26
  322.6 6.5 fusion.24
  331.2 7.3 collective-permute-done.12
  340.1 15.6 %collective-permute-done.13 = bf16[2,256,1152]{2,1,0:T(8,128)(2,1)S(1)} collective-permute-done((bf16[2,256,1152]{2,1,0:T(8,128)(2,1)S(1)}, bf16[2,256,1152]{2,1,0:T(8,128)(2,1)S(1)}, u32[]{:S(2)}, u32[]{:S(2)}) %collective-permute-start.13) | collective-permute-done | bytes 1179680 | tf_op jit(solution)/shard_map/ppermute | solution.py:16
  364.4 3.7 convolution_convert_fusion.5
  369.7 5.0 fusion.197
  377.8 7.8 collective-permute-done.6
  393.8 9.9 collective-permute-done.7
  416.2 6.6 collective-permute-done.8
  427.7 13.0 %collective-permute-done.9 = bf16[2,256,1152]{2,1,0:T(8,128)(2,1)S(1)} collective-permute-done((bf16[2,256,1152]{2,1,0:T(8,128)(2,1)S(1)}, bf16[2,256,1152]{2,1,0:T(8,128)(2,1)S(1)}, u32[]{:S(2)}, u32[]{:S(2)}) %collective-permute-start.9) | collective-permute-done | bytes 1179680 | tf_op jit(solution)/shard_map/ppermute | solution.py:16
  445.6 9.4 fusion.93
  459.5 9.8 convolution_convert_fusion.2
  470.9 10.7 convolution_convert_fusion.1
  482.9 12.3 %convolution_convert_fusion = bf16[4608,1152]{1,0:T(8,128)(2,1)} fusion(bf16[512,4608]{1,0:T(8,128)(2,1)} %multiply_convert_fusion, bf16[512,1152]{1,0:T(8,128)(2,1)S(1)} %copy-done.71), kind=kOutput, calls=%fused_computation.2 | convolution fusion | flops 5441126400 | bytes 16515072 | tf_op jit(solution)/shard_map/nf,nd->fd/dot_general | solution.py:196
  499.3 30.6 %reduce-scatter.13.cloned.1.call-done = bf16[144,1152]{1,0:T(8,128)(2,1)} async-done(((bf16[1152,1152]{1,0:T(8,128)(2,1)}), bf16[144,1152]{1,0:T(8,128)(2,1)}) %reduce-scatter.13.cloned.1.call-update) | async-done | bytes 331792 | tf_op jit(solution)/shard_map/reduce_scatter | solution.py:315
  530.0 145.1 %reduce-scatter.11.cloned.1.call-done = bf16[144,3456]{1,0:T(8,128)(2,1)} async-done(((bf16[1152,3456]{1,0:T(8,128)(2,1)}), bf16[144,3456]{1,0:T(8,128)(2,1)}) %reduce-scatter.11.cloned.1.call-update) | async-done | bytes 995344 | tf_op jit(solution)/shard_map/reduce_scatter | solution.py:306
  675.1 183.0 %reduce-scatter.15.cloned.1.call-done = bf16[144,4608]{1,0:T(8,128)(2,1)} async-done(((bf16[1152,4608]{1,0:T(8,128)(2,1)}), bf16[144,4608]{1,0:T(8,128)(2,1)}) %reduce-scatter.15.cloned.1.call-update) | async-done | bytes 1327120 | tf_op jit(solution)/shard_map/reduce_scatter | solution.py:321
  858.0 182.5 %reduce-scatter.17.cloned.1.call-done = bf16[576,1152]{1,0:T(8,128)(2,1)} async-done(((bf16[4608,1152]{1,0:T(8,128)(2,1)}), bf16[576,1152]{1,0:T(8,128)(2,1)}) %reduce-scatter.17.cloned.1.call-update) | async-done | bytes 1327120 | tf_op jit(solution)/shard_map/reduce_scatter | solution.py:324
  1051.0 40.6 %all-reduce.2 = (f32[16,63]{1,0:T(8,128)}, f32[16,63]{1,0:T(8,128)}, f32[4]{0:T(128)S(1)}) all-reduce(f32[16,63]{1,0:T(8,128)S(1)} %convolution_bitcast_fusion.5, f32[16,63]{1,0:T(8,128)S(1)} %convolution_bitcast_fusion.4, f32[4]{0:T(128)S(1)} %pad_maximum_fusion.16), channel_id=1, replica_groups=mesh['img'=8,'seq'=4] {'img','seq'}, use_global_device_ids=true, to_apply=%region_47.48 | all-reduce | flops 2020 | bytes 16160 | tf_op jit(solution)/shard_map/psum | solution.py:347
  1093.4 21.3 %all-reduce.3 = (bf16[1152]{0:T(1024)(128)(2,1)S(1)}, bf16[1152]{0:T(1024)(128)(2,1)S(1)}) all-reduce(bf16[1152]{0:T(1024)(128)(2,1)S(1)} %get-tuple-element.80, bf16[1152]{0:T(1024)(128)(2,1)S(1)} %get-tuple-element.85), channel_id=2, replica_groups=mesh['img'=8,'seq'=4] {'img'}, use_global_device_ids=true, to_apply=%region_39.40.clone | all-reduce | flops 2304 | bytes 9216
  1114.8 6.1 all-reduce.4
  1122.1 25.6 %all-reduce.8.cloned.1.call-done = (bf16[144,1152]{0,1:T(8,128)(2,1)}, bf16[144,1152]{0,1:T(8,128)(2,1)}, bf16[144,3456]{1,0:T(8,128)(2,1)}, bf16[144,1152]{1,0:...) async-done(((bf16[144,1152]{0,1:T(8,128)(2,1)}, bf16[144,1152]{0,1:T(8,128)(2,1)}, bf16[144,3456]{1,0:T(8,128)(2,1)}, bf16[144,1152]{1,0:T(8,128)(2,1)}, ...) | async-done | bytes 4644880 | tf_op jit(solution)/shard_map/psum | solution.py:340
  (438 shorter events, 202.4 us)
Async XLA Ops:
  7.2 143.0 %copy-start = (bf16[1152,1152]{1,0:T(8,128)(2,1)S(1)}, bf16[1152,1152]{1,0:T(8,128)(2,1)}, u32[]{:S(2)}) copy-start(bf16[1152,1152]{1,0:T(8,128)(2,1)} %param.25) | copy-start | bytes 7962628
  7.2 488.1 %reduce-scatter.19.cloned.1.call-start = ((), (), s32[]{:S(2)}) async-start(), calls=%async_computation.10 | async-start | bytes 2985984
  23.6 40.4 %collective-permute-start = (bf16[2,256,1152]{2,1,0:T(8,128)(2,1)}, bf16[2,256,1152]{2,1,0:T(8,128)(2,1)}, u32[]{:S(2)}, u32[]{:S(2)}) collective-permute-start(bf16[2,256,1152]{2,1,0:T(8,128)(2,1)} %slice.70), channel_id=1, source_target_pairs={{3,0},{0,1},{1,2},{2,3},{7,4},{4,5},{5,6},{6,7},{11,8},{8,9},{9,10... | collective-permute-start | bytes 3538952 | tf_op jit(solution)/shard_map/ppermute | solution.py:16
  24.0 23.1 %copy-start.93 = (s32[256]{0:T(256)}, s32[256]{0:T(256)S(1)}, u32[]{:S(2)}) copy-start(s32[256]{0:T(256)S(1)} %iota_add_fusion.4) | copy-start | bytes 3076
  24.4 18.0 %copy-start.87 = (s32[2,256]{1,0:T(2,128)}, s32[2,256]{1,0:T(2,128)S(1)}, u32[]{:S(2)}) copy-start(s32[2,256]{1,0:T(2,128)S(1)} %broadcast_minimum_fusion.4) | copy-start | bytes 6148
  31.5 38.2 %collective-permute-start.1 = (bf16[2,256,1152]{2,1,0:T(8,128)(2,1)}, bf16[2,256,1152]{2,1,0:T(8,128)(2,1)}, u32[]{:S(2)}, u32[]{:S(2)}) collective-permute-start(bf16[2,256,1152]{2,1,0:T(8,128)(2,1)} %fusion.66), channel_id=1, source_target_pairs={{3,0},{0,1},{1,2},{2,3},{7,4},{4,5},{5,6},{6,7},{11,8},{8,9},{9,10... | collective-permute-start | bytes 3538952 | tf_op jit(solution)/shard_map/ppermute | solution.py:16
  34.4 12.8 %copy-start.99 = (s32[2]{0:T(128)}, s32[2]{0:T(128)S(1)}, u32[]{:S(2)}) copy-start(s32[2]{0:T(128)S(1)} %slice_reduce_fusion) | copy-start | bytes 28
  35.0 92.1 %copy-start.44 = (pred[2,256,256]{1,2,0:T(8,128)(4,1)}, pred[2,256,256]{1,2,0:T(8,128)(4,1)S(1)}, u32[]{:S(2)}) copy-start(pred[2,256,256]{1,2,0:T(8,128)(4,1)S(1)} %get-tuple-element.190) | copy-start | bytes 393220
  35.0 95.3 %copy-start.42 = (pred[2,256,256]{1,2,0:T(8,128)(4,1)}, pred[2,256,256]{1,2,0:T(8,128)(4,1)S(1)}, u32[]{:S(2)}) copy-start(pred[2,256,256]{1,2,0:T(8,128)(4,1)S(1)} %get-tuple-element.191) | copy-start | bytes 393220
  35.0 98.4 %copy-start.46 = (pred[2,256,256]{1,2,0:T(8,128)(4,1)}, pred[2,256,256]{1,2,0:T(8,128)(4,1)S(1)}, u32[]{:S(2)}) copy-start(pred[2,256,256]{1,2,0:T(8,128)(4,1)S(1)} %get-tuple-element.189) | copy-start | bytes 393220
  35.0 104.2 %copy-start.62 = (pred[2,256,256]{1,2,0:T(8,128)(4,1)}, pred[2,256,256]{1,2,0:T(8,128)(4,1)S(1)}, u32[]{:S(2)}) copy-start(pred[2,256,256]{1,2,0:T(8,128)(4,1)S(1)} %get-tuple-element.192) | copy-start | bytes 393220
  35.5 27.8 %copy-start.95 = (s32[2,256]{1,0:T(2,128)}, s32[2,256]{1,0:T(2,128)S(1)}, u32[]{:S(2)}) copy-start(s32[2,256]{1,0:T(2,128)S(1)} %get-tuple-element.171) | copy-start | bytes 6148
  36.1 27.6 %copy-start.97 = (s32[2,256]{1,0:T(2,128)}, s32[2,256]{1,0:T(2,128)S(1)}, u32[]{:S(2)}) copy-start(s32[2,256]{1,0:T(2,128)S(1)} %get-tuple-element.200) | copy-start | bytes 6148
  52.1 17.7 %copy-start.89 = (f32[1,2,2,128]{3,1,2,0:T(2,128)}, f32[1,2,2,128]{3,1,2,0:T(2,128)S(1)}, u32[]{:S(2)}) copy-start(f32[1,2,2,128]{3,1,2,0:T(2,128)S(1)} %copy.338) | copy-start | bytes 6148
  64.0 16.0 %collective-permute-start.2 = (bf16[2,256,1152]{2,1,0:T(8,128)(2,1)}, bf16[2,256,1152]{2,1,0:T(8,128)(2,1)}, u32[]{:S(2)}, u32[]{:S(2)}) collective-permute-start(bf16[2,256,1152]{2,1,0:T(8,128)(2,1)} %collective-permute-done), channel_id=1, source_target_pairs={{3,0},{0,1},{1,2},{2,3},{7,4},{4,5},{5,6},{6,7},{11,8},{8,9},{9,10... | collective-permute-start | bytes 3538952 | tf_op jit(solution)/shard_map/ppermute | solution.py:16
  69.6 23.0 %collective-permute-start.3 = (bf16[2,256,1152]{2,1,0:T(8,128)(2,1)}, bf16[2,256,1152]{2,1,0:T(8,128)(2,1)}, u32[]{:S(2)}, u32[]{:S(2)}) collective-permute-start(bf16[2,256,1152]{2,1,0:T(8,128)(2,1)} %collective-permute-done.1), channel_id=1, source_target_pairs={{3,0},{0,1},{1,2},{2,3},{7,4},{4,5},{5,6},{6,7},{11,8},{8,9},{9,10... | collective-permute-start | bytes 3538952 | tf_op jit(solution)/shard_map/ppermute | solution.py:16
  71.1 9.0 copy-start.84
  80.0 25.3 %collective-permute-start.4 = (bf16[2,256,1152]{2,1,0:T(8,128)(2,1)}, bf16[2,256,1152]{2,1,0:T(8,128)(2,1)}, u32[]{:S(2)}, u32[]{:S(2)}) collective-permute-start(bf16[2,256,1152]{2,1,0:T(8,128)(2,1)} %collective-permute-done.2), channel_id=1, source_target_pairs={{3,0},{0,1},{1,2},{2,3},{7,4},{4,5},{5,6},{6,7},{11,8},{8,9},{9,10... | collective-permute-start | bytes 3538952 | tf_op jit(solution)/shard_map/ppermute | solution.py:16
  95.0 41.8 %collective-permute-start.5 = (bf16[2,256,1152]{2,1,0:T(8,128)(2,1)}, bf16[2,256,1152]{2,1,0:T(8,128)(2,1)}, u32[]{:S(2)}, u32[]{:S(2)}) collective-permute-start(bf16[2,256,1152]{2,1,0:T(8,128)(2,1)} %collective-permute-done.3), channel_id=1, source_target_pairs={{3,0},{0,1},{1,2},{2,3},{7,4},{4,5},{5,6},{6,7},{11,8},{8,9},{9,10... | collective-permute-start | bytes 3538952 | tf_op jit(solution)/shard_map/ppermute | solution.py:16
  115.6 9.1 slice-start.6
  139.2 14.8 %slice-start.12 = ((s8[10616832]{0:T(1024)(128)(4,1)}), s8[4194304]{0:T(1024)(128)(4,1)S(1)}, s32[]{:S(2)}) async-start(s8[10616832]{0:T(1024)(128)(4,1)} %bitcast.375), calls=%async_computation.25 | async-start | bytes 8388608
  139.2 14.8 %slice-start.13 = ((s8[10616832]{0:T(1024)(128)(4,1)}), s8[4194304]{0:T(1024)(128)(4,1)S(1)}, s32[]{:S(2)}) async-start(s8[10616832]{0:T(1024)(128)(4,1)} %bitcast.375), calls=%async_computation.26 | async-start | bytes 8388608
  160.7 31.3 %copy-start.30 = (f32[512,4608]{1,0:T(8,128)}, f32[512,4608]{1,0:T(8,128)S(1)}, u32[]{:S(2)}) copy-start(f32[512,4608]{1,0:T(8,128)S(1)} %fusion.188) | copy-start | bytes 28311556
  202.7 10.3 copy-start.12
  202.7 10.3 copy-start.40
  202.7 10.3 copy-start.49
  202.7 10.3 copy-start.90
  242.6 12.7 %slice-start.10 = ((s8[8388608]{0:T(1024)(128)(4,1)}), s8[4194304]{0:T(1024)(128)(4,1)S(1)}, s32[]{:S(2)}) async-start(s8[8388608]{0:T(1024)(128)(4,1)} %bitcast.317), calls=%async_computation.23 | async-start | bytes 8388608
  248.9 10.3 slice-start.2
  278.1 18.0 %collective-permute-start.10 = (bf16[2,256,1152]{2,1,0:T(8,128)(2,1)}, bf16[2,256,1152]{2,1,0:T(8,128)(2,1)}, u32[]{:S(2)}, u32[]{:S(2)}) collective-permute-start(bf16[2,256,1152]{2,1,0:T(8,128)(2,1)} %copy.291), channel_id=1, source_target_pairs={{3,0},{0,1},{1,2},{2,3},{7,4},{4,5},{5,6},{6,7},{11,8},{8,9},{9,10... | collective-permute-start | bytes 3538952 | tf_op jit(solution)/shard_map/ppermute | solution.py:16
  299.9 19.5 %collective-permute-start.11 = (bf16[2,256,1152]{2,1,0:T(8,128)(2,1)}, bf16[2,256,1152]{2,1,0:T(8,128)(2,1)}, u32[]{:S(2)}, u32[]{:S(2)}) collective-permute-start(bf16[2,256,1152]{2,1,0:T(8,128)(2,1)} %add_convert_fusion.4), channel_id=1, source_target_pairs={{3,0},{0,1},{1,2},{2,3},{7,4},{4,5},{5,6},{6,7},{11,8},{8,9},{9,10... | collective-permute-start | bytes 3538952 | tf_op jit(solution)/shard_map/ppermute | solution.py:16
  309.7 187.6 %reduce-scatter.21.cloned.1.call-start = ((), (), s32[]{:S(2)}) async-start(), calls=%async_computation.11 | async-start | bytes 2985984
  322.6 15.9 %collective-permute-start.12 = (bf16[2,256,1152]{2,1,0:T(8,128)(2,1)}, bf16[2,256,1152]{2,1,0:T(8,128)(2,1)}, u32[]{:S(2)}, u32[]{:S(2)}) collective-permute-start(bf16[2,256,1152]{2,1,0:T(8,128)(2,1)} %add_convert_fusion.3), channel_id=1, source_target_pairs={{3,0},{0,1},{1,2},{2,3},{7,4},{4,5},{5,6},{6,7},{11,8},{8,9},{9,10... | collective-permute-start | bytes 3538952 | tf_op jit(solution)/shard_map/ppermute | solution.py:16
  340.0 15.7 %collective-permute-start.13 = (bf16[2,256,1152]{2,1,0:T(8,128)(2,1)S(1)}, bf16[2,256,1152]{2,1,0:T(8,128)(2,1)S(1)}, u32[]{:S(2)}, u32[]{:S(2)}) collective-permute-start(bf16[2,256,1152]{2,1,0:T(8,128)(2,1)S(1)} %add_convert_fusion.2), channel_id=1, source_target_pairs={{3,0},{0,1},{1,2},{2,3},{7,4},{4,5},{5,6},{6,7},{11,8},{8,9},{9,10... | collective-permute-start | bytes 3538952 | tf_op jit(solution)/shard_map/ppermute | solution.py:16
  363.2 166.8 %reduce-scatter.13.cloned.1.call-start = ((), (), s32[]{:S(2)}) async-start(), calls=%async_computation.7 | async-start | bytes 2985984 | tf_op jit(solution)/shard_map/reduce_scatter | solution.py:315
  369.6 16.1 %collective-permute-start.6 = (bf16[2,256,1152]{2,1,0:T(8,128)(2,1)}, bf16[2,256,1152]{2,1,0:T(8,128)(2,1)}, u32[]{:S(2)}, u32[]{:S(2)}) collective-permute-start(bf16[2,256,1152]{2,1,0:T(8,128)(2,1)} %copy.282), channel_id=1, source_target_pairs={{3,0},{0,1},{1,2},{2,3},{7,4},{4,5},{5,6},{6,7},{11,8},{8,9},{9,10... | collective-permute-start | bytes 3538952 | tf_op jit(solution)/shard_map/ppermute | solution.py:16
  377.8 10.1 copy-start.5
  387.8 15.8 %collective-permute-start.7 = (bf16[2,256,1152]{2,1,0:T(8,128)(2,1)S(1)}, bf16[2,256,1152]{2,1,0:T(8,128)(2,1)}, u32[]{:S(2)}, u32[]{:S(2)}) collective-permute-start(bf16[2,256,1152]{2,1,0:T(8,128)(2,1)S(1)} %add_convert_fusion.7), channel_id=1, source_target_pairs={{3,0},{0,1},{1,2},{2,3},{7,4},{4,5},{5,6},{6,7},{11,8},{8,9},{9,10... | collective-permute-start | bytes 3538952 | tf_op jit(solution)/shard_map/ppermute | solution.py:16
  393.8 13.1 %copy-start.3 = (bf16[2,16,256,256]{2,3,1,0:T(8,128)(2,1)S(1)}, bf16[2,16,256,256]{2,3,1,0:T(8,128)(2,1)}, u32[]{:S(2)}) copy-start(bf16[2,16,256,256]{2,3,1,0:T(8,128)(2,1)} %multiply_convert_fusion.1) | copy-start | bytes 12582916
  406.9 15.9 %collective-permute-start.8 = (bf16[2,256,1152]{2,1,0:T(8,128)(2,1)}, bf16[2,256,1152]{2,1,0:T(8,128)(2,1)}, u32[]{:S(2)}, u32[]{:S(2)}) collective-permute-start(bf16[2,256,1152]{2,1,0:T(8,128)(2,1)} %add_convert_fusion.6), channel_id=1, source_target_pairs={{3,0},{0,1},{1,2},{2,3},{7,4},{4,5},{5,6},{6,7},{11,8},{8,9},{9,10... | collective-permute-start | bytes 3538952 | tf_op jit(solution)/shard_map/ppermute | solution.py:16
  416.2 8.9 copy-start.104
  416.2 9.0 copy-start.19
  416.2 258.9 %reduce-scatter.11.cloned.1.call-start = ((), (), s32[]{:S(2)}) async-start(), calls=%async_computation.6 | async-start | bytes 8957952 | tf_op jit(solution)/shard_map/reduce_scatter | solution.py:306
  425.0 15.7 %collective-permute-start.9 = (bf16[2,256,1152]{2,1,0:T(8,128)(2,1)S(1)}, bf16[2,256,1152]{2,1,0:T(8,128)(2,1)S(1)}, u32[]{:S(2)}, u32[]{:S(2)}) collective-permute-start(bf16[2,256,1152]{2,1,0:T(8,128)(2,1)S(1)} %add_convert_fusion.5), channel_id=1, source_target_pairs={{3,0},{0,1},{1,2},{2,3},{7,4},{4,5},{5,6},{6,7},{11,8},{8,9},{9,10... | collective-permute-start | bytes 3538952 | tf_op jit(solution)/shard_map/ppermute | solution.py:16
  426.3 17.9 %copy-start.34 = (bf16[2,256,1152]{2,1,0:T(8,128)(2,1)S(1)}, bf16[2,256,1152]{2,1,0:T(8,128)(2,1)}, u32[]{:S(2)}) copy-start(bf16[2,256,1152]{2,1,0:T(8,128)(2,1)} %copy-done.33) | copy-start | bytes 3538948
  469.3 388.8 %reduce-scatter.15.cloned.1.call-start = ((), (), s32[]{:S(2)}) async-start(), calls=%async_computation.8 | async-start | bytes 11943936 | tf_op jit(solution)/shard_map/reduce_scatter | solution.py:321
  481.6 558.9 %reduce-scatter.17.cloned.1.call-start = ((), (), s32[]{:S(2)}) async-start(), calls=%async_computation.9 | async-start | bytes 11943936 | tf_op jit(solution)/shard_map/reduce_scatter | solution.py:324
  495.2 652.5 %all-reduce.8.cloned.1.call-start = ((), (), s32[]{:S(2)}) async-start(), calls=%async_computation.12 | async-start | bytes 10321920 | tf_op jit(solution)/shard_map/psum | solution.py:340
  (97 other events, 391.8 us)
Sparse Core Ops, SparseCore 0:
  309.8 72.7 reduce-scatter.18
  387.2 69.3 reduce-scatter.20
  460.3 69.5 reduce-scatter.12
  533.9 141.1 reduce-scatter.10
  679.0 179.0 reduce-scatter.14
  861.5 179.0 reduce-scatter.16
  1044.8 102.9 all-reduce.7
where the time goes:
time: 1170 us; the launch traced here: 1160 us
  waiting for transfers between devices  636 us (54%)
  matrix products  264 us (23%)
  local copies, waits for them, and re-layouts  108 us (9%)
  blocking collectives  68.1 us (6%)
  other arithmetic  66.8 us (6%)
  between operations  17.1 us (1%)
    reduce_scatter x1, waiting for transfers between devices, per_device(): lax.psum_scatter(w_up_grad.astype(jnp.bfloat16), 'img', scatter_dimension...  183 us
    reduce_scatter x1, waiting for transfers between devices, per_device(): lax.psum_scatter(w_down_grad.astype(jnp.bfloat16), 'img', scatter_dimensi...  183 us
    reduce_scatter x1, waiting for transfers between devices, per_device(): lax.psum_scatter(w_qkv_grad.astype(jnp.bfloat16), 'img', scatter_dimensio...  145 us
    ppermute x14, waiting for transfers between devices, shifted(): return lax.ppermute(block, axis, route)  69.4 us
    psum x1, blocking collectives, per_device(): lax.psum((rel_rows_grad, rel_cols_grad, stats), ('img', 'seq'))  40.6 us
    unnamed x262, local copies, waits for them, and re-layouts  37.3 us
    dot_general x1, matrix products, per_device(): jnp.einsum('nd,fd->nf', grad_branch, w_down, preferred_element_type=jnp.f...  31.3 us
    reduce_scatter x1, waiting for transfers between devices, per_device(): lax.psum_scatter(w_proj_grad.astype(jnp.bfloat16), 'img', scatter_dimensi...  30.6 us
  transfers between devices with their start and end apart: 21, of which 14 were waited for; matrix products, arithmetic and copies ran while one was open for 22% of the time, Pallas kernels for 0%

commit v1 on v0

v1 whole, which is shorter than its diff:
```python
import functools
import math

import jax
import jax.numpy as jnp
from jax import lax
from jax.experimental import pallas as pl
from jax.experimental.pallas import tpu as pltpu
from jax.sharding import PartitionSpec as P

SIDE = 32
EPS = 1e-06
FAR = -1e30
BF = jnp.bfloat16
F32 = jnp.float32
HIGH = lax.Precision.HIGHEST
VMEM_LIMIT = 56 * 2**20
QUERY_BLOCK = 256

RC = 2 * SIDE
KEY_MASK = RC
QUERY_MASK = KEY_MASK + 16
IMAGE_HOT = QUERY_MASK + 16
FEATURES = IMAGE_HOT + 16


def dot(a, b, ca, cb):
    return lax.dot_general(a, b, (((ca,), (cb,)), ((), ())), preferred_element_type=F32)


def params(*semantics):
    return pltpu.CompilerParams(dimension_semantics=semantics, vmem_limit_bytes=VMEM_LIMIT)


def cost(flops, bytes_accessed, transcendentals=0):
    return pl.CostEstimate(
        flops=int(flops), bytes_accessed=int(bytes_accessed), transcendentals=int(transcendentals)
    )


def features_kernel(len_ref, turn_ref, base_ref, feat_ref, valid_ref, *, span):
    tokens = feat_ref.shape[1]

    def describe(shape, axis):
        index = lax.broadcasted_iota(jnp.int32, shape, axis)
        block = index // span
        pos = index - block * span
        for k in range(tokens // span):
            pos = pos + jnp.where(block == k, base_ref[k], 0)
        ends = []
        total = 0
        for j in range(4):
            total = total + len_ref[j]
            ends.append(total)
        segment = sum((pos >= ends[j]).astype(jnp.int32) for j in range(4))
        return pos, ends, segment

    pos, ends, segment = describe((1, tokens), 1)
    picked = jnp.minimum(segment, 3)
    begin = jnp.zeros_like(pos)
    length = jnp.zeros_like(pos)
    turn = jnp.zeros_like(pos)
    for j in range(4):
        here = picked == j
        begin = jnp.where(here, ends[j] - len_ref[j], begin)
        length = jnp.where(here, len_ref[j], length)
        turn = jnp.where(here, turn_ref[j], turn)
    full = length == SIDE * SIDE
    side = jnp.where(full, SIDE, SIDE // 2)
    u = pos - begin
    bits = SIDE.bit_length() - 1
    r0 = jnp.where(full, u >> bits, u >> (bits - 1))
    c0 = u & (side - 1)
    r1 = jnp.where((turn & 1) == 1, side - 1 - r0, r0)
    c1 = jnp.where(((turn >> 1) & 1) == 1, side - 1 - c0, c0)
    valid = pos < ends[3]
    row = jnp.where(valid, jnp.where(turn >= 4, c1, r1), 0)
    col = jnp.where(valid, jnp.where(turn >= 4, r1, c1), 0)
    which = lax.broadcasted_iota(jnp.int32, (SIDE, tokens), 0)
    few = lax.broadcasted_iota(jnp.int32, (16, tokens), 0)

    def put(start, value):
        feat_ref[start : start + value.shape[0], :] = value.astype(BF)

    put(0, jnp.where(which == row, 1.0, 0.0))
    put(SIDE, jnp.where(which == col, 1.0, 0.0))
    put(KEY_MASK, jnp.where(few == segment, 1.0, 0.0))
    put(QUERY_MASK, jnp.where((few < 5) & (few != segment), FAR, 0.0))
    put(IMAGE_HOT, jnp.where(few == picked, 1.0, 0.0))
    down_pos, down_ends, unused = describe(valid_ref.shape, 0)
    valid_ref[...] = jnp.where(down_pos < down_ends[3], 1.0, 0.0)


def token_features(lengths, turns, bases, span, mine):
    tokens = bases.shape[0] * span
    smem = pl.BlockSpec(memory_space=pltpu.SMEM)
    return pl.pallas_call(
        functools.partial(features_kernel, span=span),
        out_shape=(
            jax.ShapeDtypeStruct((FEATURES, tokens), BF),
            jax.ShapeDtypeStruct((mine, 128), F32),
        ),
        in_specs=[smem, smem, smem],
        name="token_features",
    )(lengths, turns, bases)


def stack_heads(ref):
    return jnp.concatenate([ref[p, 0].astype(F32) for p in range(ref.shape[0])], axis=0).astype(BF)


def forward_kernel(a_ref, w_ref, time_ref, table_ref, feat_ref, qkv_ref, o_ref, lse_ref, *, scale):
    width = w_ref.shape[2]
    tokens = a_ref.shape[1]
    qkv = jnp.dot(stack_heads(w_ref), a_ref[...], preferred_element_type=F32)
    hot = feat_ref[IMAGE_HOT:, :].astype(F32)

    def timed(k):
        return sum(time_ref[k, 0][:, j : j + 1] * hot[j : j + 1] for j in range(4))

    q = ((qkv[:width] + timed(0)) * scale).astype(BF)
    k = qkv[width : 2 * width].astype(BF)
    v = (qkv[2 * width :] + timed(1)).astype(BF)
    qkv_ref[0, 0] = q
    qkv_ref[1, 0] = k
    qkv_ref[2, 0] = v
    bias = jnp.dot(table_ref[0], feat_ref[:RC], preferred_element_type=F32).astype(BF)
    key = jnp.concatenate([feat_ref[:QUERY_MASK], k], axis=0).T
    for b in range(tokens // QUERY_BLOCK):
        at = slice(b * QUERY_BLOCK, (b + 1) * QUERY_BLOCK)
        query = jnp.concatenate(
            [bias[:, at], feat_ref[QUERY_MASK:IMAGE_HOT, at], q[:, at]], axis=0
        )
        s = jnp.dot(key, query, preferred_element_type=F32)
        top = jnp.max(s, axis=0, keepdims=True)
        e = jnp.exp(s - top)
        total = jnp.sum(e, axis=0, keepdims=True)
        o = jnp.dot(v, e.astype(BF), preferred_element_type=F32) / total
        o_ref[0, :, at] = o.astype(BF)
        lse_ref[0, :, at] = top + jnp.log(total)


def attend_forward(attn_t, w_heads, times, tables, feats, scale):
    parts, heads, width, dm = w_heads.shape
    tokens = attn_t.shape[1]
    whole = lambda h: (0, 0)
    return pl.pallas_call(
        functools.partial(forward_kernel, scale=scale),
        grid=(heads,),
        in_specs=[
            pl.BlockSpec(attn_t.shape, whole),
            pl.BlockSpec((parts, 1, width, dm), lambda h: (0, h, 0, 0)),
            pl.BlockSpec((2, 1, width, 4), lambda h: (0, h, 0, 0)),
            pl.BlockSpec((1, RC, RC), lambda h: (h, 0, 0)),
            pl.BlockSpec(feats.shape, whole),
        ],
        out_specs=[
            pl.BlockSpec((parts, 1, width, tokens), lambda h: (0, h, 0, 0)),
            pl.BlockSpec((1, width, tokens), lambda h: (h, 0, 0)),
            pl.BlockSpec((1, 1, tokens), lambda h: (h, 0, 0)),
        ],
        out_shape=[
            jax.ShapeDtypeStruct((parts, heads, width, tokens), BF),
            jax.ShapeDtypeStruct((heads, width, tokens), BF),
            jax.ShapeDtypeStruct((heads, 1, tokens), F32),
        ],
        compiler_params=params("arbitrary"),
        cost_estimate=cost(
            2 * heads * tokens * (3 * width * dm + tokens * 512), 12e6, heads * tokens * tokens
        ),
        name="attention_forward",
    )(attn_t, w_heads, times, tables, feats)


def backward_kernel(
    qkv_ref, o_ref, do_ref, lse_ref, table_ref, feat_ref, d_ref, toe_ref, image_ref, *, scale
):
    width = o_ref.shape[1]
    tokens = o_ref.shape[2]
    q, k, v = (qkv_ref[p, 0] for p in range(3))
    do = do_ref[0]
    delta = jnp.sum(do.astype(F32) * o_ref[0].astype(F32), axis=0, keepdims=True)
    rc = feat_ref[:RC]
    bias = jnp.dot(table_ref[0], rc, preferred_element_type=F32).astype(BF)
    key_t = jnp.concatenate([feat_ref[:QUERY_MASK], k], axis=0)
    key = key_t.T
    value = v.T
    dk = jnp.zeros((tokens, width), F32)
    dv = jnp.zeros((tokens, width), F32)
    toe = jnp.zeros((RC, RC), F32)
    dq_parts = []
    for b in range(tokens // QUERY_BLOCK):
        at = slice(b * QUERY_BLOCK, (b + 1) * QUERY_BLOCK)
        query = jnp.concatenate(
            [bias[:, at], feat_ref[QUERY_MASK:IMAGE_HOT, at], q[:, at]], axis=0
        )
        s = jnp.dot(key, query, preferred_element_type=F32)
        p = jnp.exp(s - lse_ref[0, :, at])
        dp = jnp.dot(value, do[:, at], preferred_element_type=F32)
        ds = (p * (dp - delta[:, at])).astype(BF)
        dq = jnp.dot(key_t, ds, preferred_element_type=F32)
        dq_parts.append((dq[QUERY_MASK:] * scale).astype(BF))
        high = dq[:RC].astype(BF)
        low = (dq[:RC] - high.astype(F32)).astype(BF)
        toe = toe + dot(rc[:, at], high, 1, 1) + dot(rc[:, at], low, 1, 1)
        dk = dk + dot(ds, q[:, at], 1, 1)
        dv = dv + dot(p.astype(BF), do[:, at], 1, 1)
    dq = jnp.concatenate(dq_parts, axis=1)
    dk = dk.T.astype(BF)
    dv = dv.T.astype(BF)
    d_ref[0, 0] = dq
    d_ref[1, 0] = dk
    d_ref[2, 0] = dv
    toe_ref[0] = toe
    hot = feat_ref[IMAGE_HOT:]
    image_ref[0, 0] = dot(dq, hot, 1, 1)
    image_ref[1, 0] = dot(dv, hot, 1, 1)


def attend_backward(qkv, o, do, lse, tables, feats, scale, first, count):
    parts, heads, width, tokens = qkv.shape
    head3 = lambda h: (first + h, 0, 0)
    head4 = lambda h: (0, first + h, 0, 0)
    return pl.pallas_call(
        functools.partial(backward_kernel, scale=scale),
        grid=(count,),
        in_specs=[
            pl.BlockSpec((parts, 1, width, tokens), head4),
            pl.BlockSpec((1, width, tokens), head3),
            pl.BlockSpec((1, width, tokens), head3),
            pl.BlockSpec((1, 1, tokens), head3),
            pl.BlockSpec((1, RC, RC), head3),
            pl.BlockSpec(feats.shape, lambda h: (0, 0)),
        ],
        out_specs=[
            pl.BlockSpec((parts, 1, width, tokens), lambda h: (0, h, 0, 0)),
            pl.BlockSpec((1, RC, RC), lambda h: (h, 0, 0)),
            pl.BlockSpec((2, 1, width, 16), lambda h: (0, h, 0, 0)),
        ],
        out_shape=[
            jax.ShapeDtypeStruct((parts, count, width, tokens), BF),
            jax.ShapeDtypeStruct((count, RC, RC), F32),
            jax.ShapeDtypeStruct((2, count, width, 16), F32),
        ],
        compiler_params=params("arbitrary"),
        cost_estimate=cost(
            2 * count * tokens * tokens * 5 * 256, 2e6 * count, count * tokens * tokens
        ),
        name="attention_backward",
    )(qkv, o, do, lse, tables, feats)


def mlp_kernel(
    tile_ref, m_ref, mt_ref, g_ref, up_ref, down_ref, two_ref, gm_ref,
    two_out, gm_out, send_ref, own_ref, wd_ref,
):
    step = pl.program_id(0)

    @pl.when(step == 0)
    def _():
        two_out[...] = two_ref[...]
        gm_out[...] = gm_ref[...]

    up = jnp.dot(m_ref[...], up_ref[...], preferred_element_type=F32)
    half = 0.5 + 0.5 * lax.erf(up * math.sqrt(0.5))
    slope = half + up * (jnp.exp(-0.5 * up * up) * (1.0 / math.sqrt(2.0 * math.pi)))
    act = (up * half).astype(BF)
    two_out[...] += jnp.dot(act, down_ref[...], preferred_element_type=F32)
    du = (dot(g_ref[...], down_ref[...], 1, 1) * slope).astype(BF)
    gm_out[...] += dot(du, up_ref[...], 1, 1)
    wd_ref[...] = dot(act, g_ref[...], 0, 0).astype(BF)
    wu = jnp.dot(mt_ref[...], du, preferred_element_type=F32).astype(BF)

    @pl.when(step == 0)
    def _():
        send_ref[...] = wu

    @pl.when(step == 1)
    def _():
        own_ref[...] = wu


def mlp(tiles, m, mt, g, w_up, w_down, two, gm, tile):
    rows, dm = m.shape
    whole = lambda i, t: (0, 0)
    return pl.pallas_call(
        mlp_kernel,
        grid_spec=pltpu.PrefetchScalarGridSpec(
            num_scalar_prefetch=1,
            grid=(2,),
            in_specs=[
                pl.BlockSpec((rows, dm), whole),
                pl.BlockSpec((dm, rows), whole),
                pl.BlockSpec((rows, dm), whole),
                pl.BlockSpec((dm, tile), lambda i, t: (0, t[i])),
                pl.BlockSpec((tile, dm), lambda i, t: (t[i], 0)),
                pl.BlockSpec((rows, dm), whole),
                pl.BlockSpec((rows, dm), whole),
            ],
            out_specs=[
                pl.BlockSpec((rows, dm), whole),
                pl.BlockSpec((rows, dm), whole),
                pl.BlockSpec((dm, tile), whole),
                pl.BlockSpec((dm, tile), whole),
                pl.BlockSpec((tile, dm), lambda i, t: (lax.rem(t[i], 2), 0)),
            ],
        ),
        out_shape=[
            jax.ShapeDtypeStruct((rows, dm), F32),
            jax.ShapeDtypeStruct((rows, dm), F32),
            jax.ShapeDtypeStruct((dm, tile), BF),
            jax.ShapeDtypeStruct((dm, tile), BF),
            jax.ShapeDtypeStruct((2 * tile, dm), BF),
        ],
        compiler_params=params("arbitrary"),
        cost_estimate=cost(24 * rows * dm * tile, 25e6, 2 * rows * tile),
        name="feed_forward",
    )(tiles, m, mt, g, w_up, w_down, two, gm)


def ring_order(count):
    return list(range(0, count, 2)) + list(range(1, count, 2))[::-1]


def ring_reduce(job, direction, count):
    order = ring_order(count)
    place = [order.index(i) for i in range(count)]
    route = [(order[p], order[(p + direction) % count]) for p in range(count)]
    me = jnp.asarray(place, jnp.int32)[lax.axis_index("img")]
    table = jnp.asarray(order, jnp.int32)
    moving = None
    for step in range(count):
        chunk = table[(me - direction * (1 + step)) % count]
        term = job(chunk)
        total = term if moving is None else moving.astype(F32) + term
        if step == count - 1:
            return total
        moving = lax.ppermute(total.astype(BF), "img", route)


def pick(array, index, axis=0):
    return lax.dynamic_index_in_dim(array, index, axis, keepdims=False)


def mean(x):
    return jnp.mean(x, axis=-1, keepdims=True)


def normalised(x):
    centre = x - mean(x)
    root = lax.rsqrt(mean(centre * centre) + EPS)
    return centre * root, root


def norm_backward(d, n, root):
    return root * (d - mean(d) - n * mean(d * n))


def toeplitz_tables(rel, count):
    d = jnp.arange(2 * count - 1, dtype=jnp.int32)
    t = jnp.arange(count, dtype=jnp.int32)
    hot = (d[:, None, None] == t[None, None, :] - t[None, :, None] + count - 1).astype(BF)
    return jnp.einsum("hd,dtr->htr", rel.astype(BF), hot, preferred_element_type=F32)


def per_device(
    tokens, time_embed, image_lengths, grid_turns, ln1_gain, w_qkv, w_time_q, time_value_weight,
    rel_rows, rel_cols, output_projection_weight, ln2_gain, w_up, w_down, out_grad,
):
    slots, span, dm = tokens.shape
    heads = rel_rows.shape[0]
    width = dm // heads
    ff = w_up.shape[1]
    scale = width ** (-0.5)
    n_seq = lax.axis_size("seq")
    n_img = lax.axis_size("img")
    cores = n_seq // slots
    own_heads = heads // cores
    cols = own_heads * width
    me_img = lax.axis_index("img")
    me_seq = lax.axis_index("seq")
    y = me_seq // cores
    c = me_seq % cores
    mine = slots * span
    over_y = [(s, (slots - 1 - s // cores) * cores + s % cores) for s in range(n_seq)]
    over_core = [(s, s // cores * cores + cores - 1 - s % cores) for s in range(n_seq)]

    def swap_y(a):
        return lax.ppermute(a, "seq", over_y)

    def swap_core(a):
        return lax.ppermute(a, "seq", over_core)

    tok_own = pick(tokens, y)
    tok_rx = swap_y(pick(tokens, 1 - y))
    grad_own = pick(out_grad, y)
    grad_rx = swap_y(pick(out_grad, 1 - y))
    block = lambda yy, cc: (yy * cores + cc) * span
    bases = jnp.stack([block(y, c), block(1 - y, c), block(y, 1 - c), block(1 - y, 1 - c)])
    feats, valid = token_features(
        pick(image_lengths, y), pick(grid_turns, y), bases.astype(jnp.int32), span, mine
    )
    valid = valid[:, :1]

    x = jnp.concatenate([tok_own, tok_rx], axis=0).astype(F32)
    n_one, root_one = normalised(x)
    attn_mine = (n_one * ln1_gain).astype(BF)
    attn_sib = swap_core(attn_mine)
    attn_in = jnp.concatenate([attn_mine, attn_sib], axis=0)

    w_heads = pick(w_qkv.reshape(dm, 3, cores, own_heads, width), c, 2)
    w_heads = jnp.transpose(w_heads, (1, 2, 3, 0))
    te = pick(time_embed, y)
    time_pair = jnp.stack(
        [
            dot(lax.dynamic_slice_in_dim(w, c * cols, cols, 1), te, 0, 1)
            for w in (w_time_q, time_value_weight)
        ]
    ).reshape(2, own_heads, width, 4)
    te_all = lax.all_gather(time_embed, "img")
    row_table = toeplitz_tables(lax.dynamic_slice_in_dim(rel_rows, c * own_heads, own_heads), SIDE)
    col_table = toeplitz_tables(lax.dynamic_slice_in_dim(rel_cols, c * own_heads, own_heads), SIDE)
    gap = jnp.zeros_like(row_table)
    tables = jnp.concatenate(
        [
            jnp.concatenate([row_table, gap], axis=2),
            jnp.concatenate([gap, col_table], axis=2),
        ],
        axis=1,
    ).astype(BF)

    qkv, o_own, lse = attend_forward(attn_in.T, w_heads, time_pair, tables, feats, scale)

    o_far = swap_core(o_own).reshape(cols, 2 * mine)
    o_flat = o_own.reshape(cols, 2 * mine)
    o_far = jnp.concatenate([o_far[:, mine:], o_far[:, :mine]], axis=1)
    attn_all = jnp.concatenate(
        [jnp.where(c == 0, o_flat, o_far), jnp.where(c == 0, o_far, o_flat)], axis=0
    )
    branch_one = dot(attn_all[:, :mine], output_projection_weight, 0, 0)
    hidden_one = x + branch_one
    n_two, root_two = normalised(hidden_one)
    mlp_in = (n_two * ln2_gain).astype(BF)
    grad_two = jnp.concatenate([grad_own, grad_rx], axis=0).astype(F32) * valid
    grad_branch = grad_two.astype(BF)

    tile = ff // 4
    zero = jnp.zeros((mine, dm), F32)
    mlp_in_t = mlp_in.T
    pair = jnp.stack([1 - c, c]).astype(jnp.int32)
    two, gm, send_a, own_a, down_a = mlp(
        pair, mlp_in, mlp_in_t, grad_branch, w_up, w_down, zero, zero, tile
    )
    two, gm, send_b, own_b, down_b = mlp(
        2 + pair, mlp_in, mlp_in_t, grad_branch, w_up, w_down, two, gm, tile
    )
    rx_a = swap_core(send_a)
    rx_b = swap_core(send_b)
    low = ff // n_img // cores
    down = jnp.concatenate([down_a, down_b], axis=0).reshape(n_img, cores, low, dm)
    down_rx = swap_core(pick(down, 1 - c, 1))
    rows = dm // n_img

    def up_job(own, rx):
        own = own.reshape(n_img, rows, tile)
        rx = rx.reshape(n_img, rows, tile)
        return lambda i: pick(own, i).astype(F32) + pick(rx, i).astype(F32)

    def down_job(start, size):
        def term(i):
            at = lax.dynamic_slice(down, (i, c, start, 0), (1, 1, size, dm)).reshape(size, dm)
            far = lax.dynamic_slice(down_rx, (i, start, 0), (1, size, dm)).reshape(size, dm)
            return at.astype(F32) + far.astype(F32)

        return term

    up_a = ring_reduce(up_job(own_a, rx_a), 1, n_img)
    up_b = ring_reduce(up_job(own_b, rx_b), 1, n_img)
    down_lo = ring_reduce(down_job(0, low // 2), -1, n_img)
    down_hi = ring_reduce(down_job(low // 2, low // 2), -1, n_img)

    hidden_two = hidden_one + two
    output = (hidden_two * valid).astype(BF)
    stats = jnp.stack(
        [
            jnp.sum(valid * hidden_two * hidden_two),
            jnp.sum(valid * branch_one * branch_one),
            jnp.sum(valid * two * two),
            jnp.sum(valid),
        ]
    )
    ln2_grad = jnp.sum(gm * n_two, axis=0)
    grad_one = grad_two + norm_backward(gm * ln2_gain, n_two, root_two)
    gb_mine = grad_one.astype(BF)
    gb_all = jnp.concatenate([gb_mine, swap_core(gb_mine)], axis=0)
    w_proj_rows = lax.dynamic_slice_in_dim(output_projection_weight, c * cols, cols, 0)
    do = dot(w_proj_rows, gb_all, 1, 1).astype(BF).reshape(own_heads, width, 2 * mine)
    gb_cols = lax.dynamic_slice_in_dim(gb_all, c * cols, cols, 1)
    proj_part = dot(attn_all, gb_cols, 1, 0).astype(BF).reshape(n_img, rows, cols)
    proj = ring_reduce(lambda i: pick(proj_part, i).astype(F32), 1, n_img)

    group = 2
    pieces = [
        attend_backward(qkv, o_own, do, lse, tables, feats, scale, h, group)
        for h in range(0, own_heads, group)
    ]
    d = jnp.concatenate([p[0] for p in pieces], axis=1).reshape(3, cols, 2 * mine)
    toe = jnp.concatenate([p[1] for p in pieces], axis=0)
    image_grads = jnp.concatenate([p[2] for p in pieces], axis=1)[..., :4]

    w_v_part = dot(attn_in, d[2], 0, 1).astype(BF).reshape(n_img, rows, cols)
    w_qk_part = dot(attn_in, d[:2].reshape(2 * cols, 2 * mine), 0, 1)
    w_qk_part = w_qk_part.astype(BF).reshape(n_img, rows, 2 * cols)
    w_v = ring_reduce(lambda i: pick(w_v_part, i).astype(F32), 1, n_img)
    w_qk = ring_reduce(lambda i: pick(w_qk_part, i).astype(F32), -1, n_img)

    back = dot(d.reshape(3 * cols, 2 * mine), w_heads.reshape(3 * cols, dm), 0, 0)
    back = back[:mine] + swap_core(back[mine:].astype(BF)).astype(F32)
    ln1_grad = jnp.sum(back * n_one, axis=0)
    input_grad = (grad_one + norm_backward(back * ln1_gain, n_one, root_one)).astype(BF)

    def returned(a):
        own, far = a[:span], swap_y(a[span:])
        return jnp.stack([jnp.where(y == 0, own, far), jnp.where(y == 0, far, own)])

    output = returned(output)
    input_grad = returned(input_grad)

    images = lax.all_gather(image_grads.reshape(2, cols, 4), ("img", "seq"))
    images = images.reshape(n_img, slots, cores, 2, cols, 4)
    images = jnp.transpose(images, (3, 0, 1, 5, 2, 4)).reshape(2, n_img * slots * 4, dm)
    te_rows = lax.dynamic_slice_in_dim(te_all.reshape(n_img * slots * 4, dm), me_img * rows, rows, 1)
    te_rows = te_rows.astype(F32)
    w_time_q_grad = lax.dot_general(te_rows, images[0], (((0,), (0,)), ((), ())), precision=HIGH)
    w_time_v_grad = lax.dot_general(te_rows, images[1], (((0,), (0,)), ((), ())), precision=HIGH)

    reach = jnp.arange(2 * SIDE - 1, dtype=jnp.int32)
    side = jnp.arange(SIDE, dtype=jnp.int32)
    diag = (reach == side[:, None, None] - side[None, :, None] + SIDE - 1).astype(F32)
    rel = jnp.stack([toe[:, :SIDE, :SIDE], toe[:, SIDE:, SIDE:]])
    rel = jnp.einsum("khrt,rtd->khd", rel, diag, precision=HIGH)
    rel_all = lax.dynamic_update_slice(
        jnp.zeros((2, heads, 2 * SIDE - 1), F32), rel, (0, c * own_heads, 0)
    )
    small = jnp.concatenate([ln1_grad, ln2_grad, rel_all.reshape(-1), stats])
    small = lax.psum(small, ("img", "seq"))
    ln1_gain_grad = lax.dynamic_slice_in_dim(small, me_img * rows, rows)
    ln2_gain_grad = lax.dynamic_slice_in_dim(small, dm + me_img * rows, rows)
    rel_all = small[2 * dm : -4].reshape(2, heads, 2 * SIDE - 1)
    rms_values = jnp.sqrt(small[-4:-1] / (small[-1] * dm))

    def finish(part):
        part = part.astype(BF)
        part = (part.astype(F32) + swap_y(part).astype(F32)).astype(BF)
        far = swap_core(part)
        first = jnp.where(c == 0, part, far).astype(F32)
        second = jnp.where(c == 0, far, part).astype(F32)
        return first, second

    ups = finish(up_a) + finish(up_b)
    w_up_grad = jnp.concatenate(ups, axis=1)
    d0, d1 = finish(jnp.concatenate([down_lo, down_hi], axis=0))
    w_down_grad = jnp.concatenate([d0, d1], axis=0)
    w_proj_grad = jnp.concatenate(finish(proj), axis=1)
    v0, v1 = finish(w_v)
    q0, q1 = finish(w_qk)
    w_qkv_grad = jnp.concatenate([q0[:, :cols], q1[:, :cols], q0[:, cols:], q1[:, cols:], v0, v1], axis=1)
    return (
        output,
        input_grad,
        ln1_gain_grad,
        w_qkv_grad,
        w_time_q_grad,
        w_time_v_grad,
        rel_all[0],
        rel_all[1],
        w_proj_grad,
        ln2_gain_grad,
        w_up_grad,
        w_down_grad,
        rms_values,
    )


def solution(mesh):
    return jax.shard_map(
        per_device,
        mesh=mesh,
        in_specs=(
            P("img", "seq", None),
            P("img", None, None),
            P("img", None),
            P("img", None),
        )
        + (P(),) * 10
        + (P("img", "seq", None),),
        out_specs=(
            P("img", "seq", None),
            P("img", "seq", None),
            P("img"),
            P("img", None),
            P("img", None),
            P("img", None),
            P(),
            P(),
            P("img", None),
            P("img"),
            P("img", None),
            P("img", None),
            P(),
        ),
        check_vma=False,
    )
```

time: 1170 us -> 756 us (0.65)
  waiting for transfers between devices: 636 us -> 188 us
  matrix products: 264 us -> 37.4 us
  Pallas kernels: 0 us -> 138 us
  blocking collectives: 68.1 us -> 114 us
  starting transfers between devices: 4.66 us -> 48.6 us
  other arithmetic: 66.8 us -> 98.5 us
  local copies, waits for them, and re-layouts: 108 us -> 76.8 us
  between operations: 17.1 us -> 44.2 us
    reduce_scatter x4 -> x0, waiting for transfers between devices: 541 us -> none  [the longest x1 183 us: per_device(): lax.psum_scatter(w_up_grad.astype(jnp.bfloat16), 'img', scatter_dimension...]
    dot_general x50 -> x13, matrix products: 264 us -> 37.4 us  [the longest x8 31.7 us: dot(): lax.dot_general(a, b, (((ca,), (cb,)), ((), ())), preferred_element_type=...]
    pallas_call x0 -> x8, Pallas kernels: none -> 138 us  [the longest x2 64.5 us: mlp(): pl.pallas_call(mlp_kernel, grid_spec=pltpu.PrefetchScalarGridSpec(num_sca...]
    ppermute x14 -> x72, waiting for transfers between devices: 69.4 us -> 188 us  [the longest x49 169 us: ring_reduce(): moving = lax.ppermute(total.astype(BF), 'img', route)]
    all_gather x0 -> x2, blocking collectives: none -> 73.9 us  [the longest x1 42.5 us: per_device(): images = lax.all_gather(image_grads.reshape(2, cols, 4), ('img', 'seq'))]
    ppermute x14 -> x72, starting transfers between devices: 4.16 us -> 48.6 us  [the longest x49 35.6 us: ring_reduce(): moving = lax.ppermute(total.astype(BF), 'img', route)]
    reshape x8 -> x2, local copies, waits for them, and re-layouts: 26.3 us -> 0.15 us  [the longest x1 0.11 us: per_device(): small = jnp.concatenate([ln1_grad, ln2_grad, rel_all.reshape(-1), stats])]
    psum x1 -> x0, waiting for transfers between devices: 25.6 us -> none  [per_device(): lax.psum(w_time_q_grad.astype(jnp.bfloat16), 'seq').astype(jnp.float32)]
  transfers between devices with their start and end apart: 21 -> 72, of which waited for: 14 -> 39; matrix products, arithmetic and copies ran while one was open for 22% -> 23% of each run, Pallas kernels for 0% -> 10%
where the time goes in v1:
time: 756 us; the launch traced here: 746 us
  waiting for transfers between devices  188 us (25%)
  Pallas kernels  138 us (18%)
  blocking collectives  114 us (15%)
  other arithmetic  98.5 us (13%)
  local copies, waits for them, and re-layouts  76.8 us (10%)
  starting transfers between devices  48.6 us (6%)
  between operations  44.2 us (6%)
  matrix products  37.4 us (5%)
    ppermute x49, waiting for transfers between devices, ring_reduce(): moving = lax.ppermute(total.astype(BF), 'img', route)  169 us
    pallas_call x2, Pallas kernels, mlp(): pl.pallas_call(mlp_kernel, grid_spec=pltpu.PrefetchScalarGridSpec(num_sca...  64.5 us
    all_gather x1, blocking collectives, per_device(): images = lax.all_gather(image_grads.reshape(2, cols, 4), ('img', 'seq'))  42.5 us
    psum x1, blocking collectives, per_device(): small = lax.psum(small, ('img', 'seq'))  39.8 us
    pallas_call x4, Pallas kernels, attend_backward(): pl.pallas_call(functools.partial(backward_kernel, scale=scale), grid=(cou...  39.8 us
    ppermute x49, starting transfers between devices, ring_reduce(): moving = lax.ppermute(total.astype(BF), 'img', route)  35.6 us
    convert_element_type x39, other arithmetic, ring_reduce(): moving = lax.ppermute(total.astype(BF), 'img', route)  33.2 us
    pallas_call x1, Pallas kernels, attend_forward(): pl.pallas_call(functools.partial(forward_kernel, scale=scale), grid=(head...  32.4 us
  transfers between devices with their start and end apart: 72, of which 39 were waited for; matrix products, arithmetic and copies ran while one was open for 23% of the time, Pallas kernels for 10%

profile of v1, /device:TPU:0, one launch (start us, length us, event | category | flops | bytes accessed | tf_op | source)
XLA Modules:
  0.0 745.9 jit_solution(13638378718070883186)
XLA Ops:
  8.4 5.3 dynamic-slice_bitcast_fusion.2
  13.7 5.9 collective-permute-done
  30.7 11.5 %copy.119 = bf16[1152,3456]{0,1:T(8,128)(2,1)} copy(bf16[1152,3456]{1,0:T(8,128)(2,1)} %param.34) | data formatting | bytes 15925248 | tf_op args[5]
  49.6 4.4 dynamic-slice_bitcast_fusion.1.w_ref
  57.2 4.3 copy.126.a_ref
  61.5 32.4 %attention_forward.1 = (bf16[3,8,72,1024]{3,2,1,0:T(8,128)(2,1)}, bf16[8,72,1024]{2,1,0:T(8,128)(2,1)}, f32[8,1,1024]{2,1,0:T(1,128)}) custom-call(bf16[1152,1024]{1,0:T(8,128)(2,1)} %copy.126.a_ref, bf16[3,8,72,1152]{3,2,1,0:T(8,128)(2,1)} %dynamic-slice_bitcast_fusion.1.w_ref, f32[2,8,72,4]{3,2,1,0:T(8,128)} %pad_maximum_fusion.14.time_ref, ...), custom_call_target="tpu_custom_call" | custom-call | flops 12666798080 | bytes 12000000 | tf_op jit(solution)/shard_map/attention_forward/pallas_call | solution.py:147
  129.9 31.4 %all-gather = bf16[16,4,1152]{2,1,0:T(4,128)(2,1)S(1)} all-gather(bf16[2,4,1152]{2,1,0:T(4,128)(2,1)S(1)} %copy-done.35), channel_id=2, replica_groups=mesh['img'=8,'seq'=4] {'img'}, dimensions={0}, use_global_device_ids=true | all-gather | bytes 165888 | tf_op jit(solution)/shard_map/all_gather | solution.py:420
  179.1 4.9 fusion.136
  191.6 32.8 %feed_forward.2 = (f32[512,1152]{1,0:T(8,128)}, f32[512,1152]{1,0:T(8,128)}, bf16[1152,1152]{1,0:T(8,128)(2,1)}, bf16[1152,1152]{1,0:T(8,128)(2,1)}, bf16[2304,1152]{1,0:T(8,128)(2,1)}) custom-call(s32[2]{0:T(128)} %get-tuple-element.86.tile_ref, bf16[512,1152]{1,0:T(8,128)(2,1)} %multiply_convert_fusion.1.m_ref, bf16[1152,512]{1,0:T(8,128)(2,1)} %copy.128.mt_ref, ...), custom_call_target="tpu_custom_call" | custom-call | flops 16307453952 | bytes 25000000 | tf_op jit(solution)/shard_map/feed_forward/pallas_call | solution.py:286
  224.4 31.8 %feed_forward.3 = (f32[512,1152]{1,0:T(8,128)}, f32[512,1152]{1,0:T(8,128)}, bf16[1152,1152]{1,0:T(8,128)(2,1)}, bf16[1152,1152]{1,0:T(8,128)(2,1)}, bf16[2304,1152]{1,0:T(8,128)(2,1)}) custom-call(s32[2]{0:T(128)} %get-tuple-element.85.tile_ref, bf16[512,1152]{1,0:T(8,128)(2,1)} %multiply_convert_fusion.1.m_ref, bf16[1152,512]{1,0:T(8,128)(2,1)} %copy.128.mt_ref, ...), custom_call_target="tpu_custom_call" | custom-call | flops 16307453952 | bytes 25000000 | tf_op jit(solution)/shard_map/feed_forward/pallas_call | solution.py:286
  256.2 5.4 fusion.17
  266.8 14.0 %pad_maximum_fusion = bf16[4608,1152]{1,0:T(8,128)(2,1)S(1)} fusion(bf16[2304,1152]{1,0:T(8,128)(2,1)S(1)} %copy-done.8, bf16[2304,1152]{1,0:T(8,128)(2,1)S(1)} %bitcast.394), kind=kLoop, calls=%fused_computation | loop fusion | flops 21233664 | bytes 21233664 | tf_op jit(solution)/shard_map/concatenate | solution.py:460
  290.9 9.8 %attention_backward.7 = (bf16[3,2,72,1024]{3,2,1,0:T(8,128)(2,1)}, f32[2,64,64]{2,1,0:T(8,128)}, f32[2,2,72,16]{3,2,1,0:T(8,128)}) custom-call(bf16[3,8,72,1024]{3,2,1,0:T(8,128)(2,1)} %get-tuple-element.47.qkv_ref, bf16[8,72,1024]{2,1,0:T(8,128)(2,1)} %get-tuple-element.41.o_ref, bf16[8,72,1024]{2,1,0:T(8,128)(2,1)} %bitcast.424, ...), custom_call_target="tpu_custom_call" | custom-call | flops 5368709120 | bytes 4000000 | tf_op jit(solution)/shard_map/attention_backward/pallas_call | solution.py:224
  300.7 9.9 %attention_backward.6 = (bf16[3,2,72,1024]{3,2,1,0:T(8,128)(2,1)}, f32[2,64,64]{2,1,0:T(8,128)}, f32[2,2,72,16]{3,2,1,0:T(8,128)}) custom-call(bf16[3,8,72,1024]{3,2,1,0:T(8,128)(2,1)} %get-tuple-element.47.qkv_ref, bf16[8,72,1024]{2,1,0:T(8,128)(2,1)} %get-tuple-element.41.o_ref, bf16[8,72,1024]{2,1,0:T(8,128)(2,1)} %bitcast.425, ...), custom_call_target="tpu_custom_call" | custom-call | flops 5368709120 | bytes 4000000 | tf_op jit(solution)/shard_map/attention_backward/pallas_call | solution.py:224
  310.6 10.2 %attention_backward.5 = (bf16[3,2,72,1024]{3,2,1,0:T(8,128)(2,1)}, f32[2,64,64]{2,1,0:T(8,128)}, f32[2,2,72,16]{3,2,1,0:T(8,128)}) custom-call(bf16[3,8,72,1024]{3,2,1,0:T(8,128)(2,1)} %get-tuple-element.47.qkv_ref, bf16[8,72,1024]{2,1,0:T(8,128)(2,1)} %get-tuple-element.41.o_ref, bf16[8,72,1024]{2,1,0:T(8,128)(2,1)} %bitcast.426, ...), custom_call_target="tpu_custom_call" | custom-call | flops 5368709120 | bytes 4000000 | tf_op jit(solution)/shard_map/attention_backward/pallas_call | solution.py:224
  320.9 9.8 %attention_backward.4 = (bf16[3,2,72,1024]{3,2,1,0:T(8,128)(2,1)}, f32[2,64,64]{2,1,0:T(8,128)}, f32[2,2,72,16]{3,2,1,0:T(8,128)}) custom-call(bf16[3,8,72,1024]{3,2,1,0:T(8,128)(2,1)} %get-tuple-element.47.qkv_ref, bf16[8,72,1024]{2,1,0:T(8,128)(2,1)} %get-tuple-element.41.o_ref, bf16[8,72,1024]{2,1,0:T(8,128)(2,1)} %bitcast.427, ...), custom_call_target="tpu_custom_call" | custom-call | flops 5368709120 | bytes 4000000 | tf_op jit(solution)/shard_map/attention_backward/pallas_call | solution.py:224
  334.4 6.8 convolution_bitcast_fusion
  352.8 42.5 %all_gather.11 = f32[32,2,576,4]{2,3,1,0:T(4,128)S(1)} all-gather(f32[1,2,576,4]{2,3,1,0:T(4,128)S(1)} %all_gather_reshape.3), channel_id=1, replica_groups=mesh['img'=8,'seq'=4] {'img','seq'}, dimensions={0}, use_global_device_ids=true | all-gather | bytes 608256 | tf_op jit(solution)/shard_map/all_gather | solution.py:529
  401.8 4.4 convolution_convert_fusion.1
  409.8 5.8 convolution_convert_fusion
  417.9 6.2 collective-permute-done.27
  424.5 5.2 collective-permute-done.18
  431.0 4.9 collective-permute-done.28
  439.0 6.3 collective-permute-done.29
  445.4 7.4 collective-permute-done.20
  453.3 5.0 collective-permute-done.30
  460.4 5.1 collective-permute-done.10
  466.3 5.8 collective-permute-done.31
  472.5 5.5 collective-permute-done.22
  478.6 4.9 collective-permute-done.32
  484.1 4.9 collective-permute-done.23
  495.5 39.8 %psum.7 = f32[4324]{0:T(1024)S(1)} all-reduce(f32[4324]{0:T(1024)S(1)} %concatenate.80), channel_id=1, replica_groups=mesh['img'=8,'seq'=4] {'img','seq'}, use_global_device_ids=true, to_apply=%region_14.15 | all-reduce | flops 4324 | bytes 34592 | tf_op jit(solution)/shard_map/psum | solution.py:546
  560.5 4.4 collective-permute-done.12
  570.6 5.4 collective-permute-done.46
  584.6 5.7 collective-permute-done.47
  593.1 4.3 collective-permute-done.38
  598.8 5.7 collective-permute-done.48
  606.1 5.5 collective-permute-done.39
  613.7 5.0 collective-permute-done.49
  630.0 5.9 collective-permute-done.56
  645.8 5.4 collective-permute-done.57
  660.7 4.6 collective-permute-done.58
  665.4 4.4 collective-permute-done.65
  679.6 5.3 collective-permute-done.66
  693.8 6.1 collective-permute-done.67
  708.7 7.1 collective-permute-done.68
  719.6 5.0 collective-permute-done.62
  730.2 10.2 %collective-permute-done.70 = bf16[288,1152]{1,0:T(8,128)(2,1)S(1)} collective-permute-done((bf16[288,1152]{1,0:T(8,128)(2,1)S(1)}, bf16[288,1152]{1,0:T(8,128)(2,1)S(1)}, u32[]{:S(2)}, u32[]{:S(2)}) %collective-permute-start.70) | collective-permute-done | bytes 663584 | tf_op jit(solution)/shard_map/ppermute | solution.py:389
  (373 shorter events, 227.2 us)
Async XLA Ops:
  3.0 16.6 %collective-permute-start = (bf16[256,1152]{1,0:T(8,128)(2,1)}, bf16[256,1152]{1,0:T(8,128)(2,1)}, u32[]{:S(2)}, u32[]{:S(2)}) collective-permute-start(bf16[256,1152]{1,0:T(8,128)(2,1)} %get-tuple-element.117), channel_id=1, source_target_pairs={{0,2},{1,3},{2,0},{3,1},{4,6},{5,7},{6,4},{7,5},{8,10},{9,11},{10,... | collective-permute-start | bytes 1769480 | tf_op jit(solution)/shard_map/ppermute | solution.py:389
  24.9 29.0 %collective-permute-start.1 = (bf16[512,1152]{1,0:T(8,128)(2,1)}, bf16[512,1152]{1,0:T(8,128)(2,1)}, u32[]{:S(2)}, u32[]{:S(2)}) collective-permute-start(bf16[512,1152]{1,0:T(8,128)(2,1)} %fusion.7), channel_id=1, source_target_pairs={{0,1},{1,0},{2,3},{3,2},{4,5},{5,4},{6,7},{7,6},{8,9},{9,8},{10,11... | collective-permute-start | bytes 3538952 | tf_op jit(solution)/shard_map/ppermute | solution.py:392
  93.9 83.1 %collective-permute-start.2 = (bf16[8,72,1024]{2,1,0:T(8,128)(2,1)}, bf16[8,72,1024]{2,1,0:T(8,128)(2,1)}, u32[]{:S(2)}, u32[]{:S(2)}) collective-permute-start(bf16[8,72,1024]{2,1,0:T(8,128)(2,1)} %get-tuple-element.41.o_ref), channel_id=1, source_target_pairs={{0,1},{1,0},{2,3},{3,2},{4,5},{5,4},{6,7},{7,6},{8,9},{9,8},{10,11... | collective-permute-start | bytes 3538952 | tf_op jit(solution)/shard_map/ppermute | solution.py:392
  95.6 78.8 %collective-permute-start.3 = (bf16[256,1152]{1,0:T(8,128)(2,1)}, bf16[256,1152]{1,0:T(8,128)(2,1)}, u32[]{:S(2)}, u32[]{:S(2)}) collective-permute-start(bf16[256,1152]{1,0:T(8,128)(2,1)} %get-tuple-element.113), channel_id=1, source_target_pairs={{0,2},{1,3},{2,0},{3,1},{4,6},{5,7},{6,4},{7,5},{8,10},{9,11},{10,... | collective-permute-start | bytes 1769480 | tf_op jit(solution)/shard_map/ppermute | solution.py:389
  224.3 329.0 %collective-permute-start.35 = (bf16[1152,1152]{1,0:T(8,128)(2,1)}, bf16[1152,1152]{1,0:T(8,128)(2,1)}, u32[]{:S(2)}, u32[]{:S(2)}) collective-permute-start(bf16[1152,1152]{1,0:T(8,128)(2,1)} %get-tuple-element.62), channel_id=1, source_target_pairs={{0,1},{1,0},{2,3},{3,2},{4,5},{5,4},{6,7},{7,6},{8,9},{9,8},{10,11... | collective-permute-start | bytes 7962632 | tf_op jit(solution)/shard_map/ppermute | solution.py:392
  261.6 25.3 %collective-permute-start.4 = (bf16[256,1152]{1,0:T(8,128)(2,1)S(1)}, bf16[256,1152]{1,0:T(8,128)(2,1)S(1)}, u32[]{:S(2)}, u32[]{:S(2)}) collective-permute-start(bf16[256,1152]{1,0:T(8,128)(2,1)S(1)} %slice.123), channel_id=1, source_target_pairs={{0,2},{1,3},{2,0},{3,1},{4,6},{5,7},{6,4},{7,5},{8,10},{9,11},{10,... | collective-permute-start | bytes 1769480 | tf_op jit(solution)/shard_map/ppermute | solution.py:389
  265.4 22.8 %collective-permute-start.5 = (bf16[512,1152]{1,0:T(8,128)(2,1)S(1)}, bf16[512,1152]{1,0:T(8,128)(2,1)S(1)}, u32[]{:S(2)}, u32[]{:S(2)}) collective-permute-start(bf16[512,1152]{1,0:T(8,128)(2,1)S(1)} %get-tuple-element.81), channel_id=1, source_target_pairs={{0,1},{1,0},{2,3},{3,2},{4,5},{5,4},{6,7},{7,6},{8,9},{9,8},{10,11... | collective-permute-start | bytes 3538952 | tf_op jit(solution)/shard_map/ppermute | solution.py:392
  265.4 289.7 %collective-permute-start.45 = (bf16[1152,1152]{1,0:T(8,128)(2,1)}, bf16[1152,1152]{1,0:T(8,128)(2,1)}, u32[]{:S(2)}, u32[]{:S(2)}) collective-permute-start(bf16[1152,1152]{1,0:T(8,128)(2,1)} %get-tuple-element.64), channel_id=1, source_target_pairs={{0,1},{1,0},{2,3},{3,2},{4,5},{5,4},{6,7},{7,6},{8,9},{9,8},{10,11... | collective-permute-start | bytes 7962632 | tf_op jit(solution)/shard_map/ppermute | solution.py:392
  286.5 337.2 %collective-permute-start.55 = (bf16[8,288,1152]{2,1,0:T(8,128)(2,1)}, bf16[8,288,1152]{2,1,0:T(8,128)(2,1)}, u32[]{:S(2)}, u32[]{:S(2)}) collective-permute-start(bf16[8,288,1152]{2,1,0:T(8,128)(2,1)} %dynamic-slice_bitcast_fusion), channel_id=1, source_target_pairs={{0,1},{1,0},{2,3},{3,2},{4,5},{5,4},{6,7},{7,6},{8,9},{9,8},{10,11... | collective-permute-start | bytes 15925256 | tf_op jit(solution)/shard_map/ppermute | solution.py:392
  351.3 64.3 %collective-permute-start.26 = (bf16[144,576]{1,0:T(8,128)(2,1)}, bf16[144,576]{1,0:T(8,128)(2,1)S(1)}, u32[]{:S(2)}, u32[]{:S(2)}) collective-permute-start(bf16[144,576]{1,0:T(8,128)(2,1)} %dynamic-slice_bitcast_fusion.9), channel_id=1, source_target_pairs={{0,8},{8,16},{16,24},{24,28},{28,20},{20,12},{12,4},{4,0},{1,9},{9... | collective-permute-start | bytes 497672 | tf_op jit(solution)/shard_map/ppermute | solution.py:338
  415.6 14.6 %collective-permute-start.8 = (bf16[144,1152]{1,0:T(8,128)(2,1)S(1)}, bf16[144,1152]{1,0:T(8,128)(2,1)S(1)}, u32[]{:S(2)}, u32[]{:S(2)}) collective-permute-start(bf16[144,1152]{1,0:T(8,128)(2,1)S(1)} %dynamic-slice_bitcast_fusion.8), channel_id=1, source_target_pairs={{0,4},{8,0},{16,8},{24,16},{28,24},{20,28},{12,20},{4,12},{1,5},{9... | collective-permute-start | bytes 995336 | tf_op jit(solution)/shard_map/ppermute | solution.py:338
  435.9 17.0 %collective-permute-start.9 = (bf16[144,1152]{1,0:T(8,128)(2,1)S(1)}, bf16[144,1152]{1,0:T(8,128)(2,1)S(1)}, u32[]{:S(2)}, u32[]{:S(2)}) collective-permute-start(bf16[144,1152]{1,0:T(8,128)(2,1)S(1)} %fusion.68), channel_id=1, source_target_pairs={{0,4},{8,0},{16,8},{24,16},{28,24},{20,28},{12,20},{4,12},{1,5},{9... | collective-permute-start | bytes 995336 | tf_op jit(solution)/shard_map/ppermute | solution.py:338
  460.4 29.0 %collective-permute-start.6 = (bf16[512,1152]{1,0:T(8,128)(2,1)}, bf16[512,1152]{1,0:T(8,128)(2,1)S(1)}, u32[]{:S(2)}, u32[]{:S(2)}) collective-permute-start(bf16[512,1152]{1,0:T(8,128)(2,1)} %slice.163), channel_id=1, source_target_pairs={{0,1},{1,0},{2,3},{3,2},{4,5},{5,4},{6,7},{7,6},{8,9},{9,8},{10,11... | collective-permute-start | bytes 3538952 | tf_op jit(solution)/shard_map/ppermute | solution.py:392
  489.1 63.1 %collective-permute-start.11 = (bf16[144,1152]{1,0:T(8,128)(2,1)}, bf16[144,1152]{1,0:T(8,128)(2,1)}, u32[]{:S(2)}, u32[]{:S(2)}) collective-permute-start(bf16[144,1152]{1,0:T(8,128)(2,1)} %fusion.66), channel_id=1, source_target_pairs={{0,4},{8,0},{16,8},{24,16},{28,24},{20,28},{12,20},{4,12},{1,5},{9... | collective-permute-start | bytes 995336 | tf_op jit(solution)/shard_map/ppermute | solution.py:338
  489.4 54.7 %collective-permute-start.33 = (bf16[144,576]{1,0:T(8,128)(2,1)S(1)}, bf16[144,576]{1,0:T(8,128)(2,1)}, u32[]{:S(2)}, u32[]{:S(2)}) collective-permute-start(bf16[144,576]{1,0:T(8,128)(2,1)S(1)} %fusion.87), channel_id=1, source_target_pairs={{0,2},{1,3},{2,0},{3,1},{4,6},{5,7},{6,4},{7,5},{8,10},{9,11},{10,... | collective-permute-start | bytes 497672 | tf_op jit(solution)/shard_map/ppermute | solution.py:389
  550.3 17.4 %collective-permute-start.7 = (bf16[256,1152]{1,0:T(8,128)(2,1)S(1)}, bf16[256,1152]{1,0:T(8,128)(2,1)S(1)}, u32[]{:S(2)}, u32[]{:S(2)}) collective-permute-start(bf16[256,1152]{1,0:T(8,128)(2,1)S(1)} %slice.127), channel_id=1, source_target_pairs={{0,2},{1,3},{2,0},{3,1},{4,6},{5,7},{6,4},{7,5},{8,10},{9,11},{10,... | collective-permute-start | bytes 1769480 | tf_op jit(solution)/shard_map/ppermute | solution.py:389
  555.1 9.8 %collective-permute-start.12 = (bf16[144,1152]{1,0:T(8,128)(2,1)S(1)}, bf16[144,1152]{1,0:T(8,128)(2,1)S(1)}, u32[]{:S(2)}, u32[]{:S(2)}) collective-permute-start(bf16[144,1152]{1,0:T(8,128)(2,1)S(1)} %fusion.65), channel_id=1, source_target_pairs={{0,4},{8,0},{16,8},{24,16},{28,24},{20,28},{12,20},{4,12},{1,5},{9... | collective-permute-start | bytes 995336 | tf_op jit(solution)/shard_map/ppermute | solution.py:338
  558.2 10.9 %collective-permute-start.36 = (bf16[144,1152]{1,0:T(8,128)(2,1)S(1)}, bf16[144,1152]{1,0:T(8,128)(2,1)S(1)}, u32[]{:S(2)}, u32[]{:S(2)}) collective-permute-start(bf16[144,1152]{1,0:T(8,128)(2,1)S(1)} %fusion.101), channel_id=1, source_target_pairs={{0,8},{8,16},{16,24},{24,28},{28,20},{20,12},{12,4},{4,0},{1,9},{9... | collective-permute-start | bytes 995336 | tf_op jit(solution)/shard_map/ppermute | solution.py:338
  559.5 16.5 %collective-permute-start.46 = (bf16[144,1152]{1,0:T(8,128)(2,1)S(1)}, bf16[144,1152]{1,0:T(8,128)(2,1)S(1)}, u32[]{:S(2)}, u32[]{:S(2)}) collective-permute-start(bf16[144,1152]{1,0:T(8,128)(2,1)S(1)} %fusion.102), channel_id=1, source_target_pairs={{0,8},{8,16},{16,24},{24,28},{28,20},{20,12},{12,4},{4,0},{1,9},{9... | collective-permute-start | bytes 995336 | tf_op jit(solution)/shard_map/ppermute | solution.py:338
  565.9 11.5 %collective-permute-start.13 = (bf16[144,1152]{1,0:T(8,128)(2,1)S(1)}, bf16[144,1152]{1,0:T(8,128)(2,1)S(1)}, u32[]{:S(2)}, u32[]{:S(2)}) collective-permute-start(bf16[144,1152]{1,0:T(8,128)(2,1)S(1)} %fusion.64), channel_id=1, source_target_pairs={{0,4},{8,0},{16,8},{24,16},{28,24},{20,28},{12,20},{4,12},{1,5},{9... | collective-permute-start | bytes 995336 | tf_op jit(solution)/shard_map/ppermute | solution.py:338
  570.2 12.9 %collective-permute-start.37 = (bf16[144,1152]{1,0:T(8,128)(2,1)S(1)}, bf16[144,1152]{1,0:T(8,128)(2,1)S(1)}, u32[]{:S(2)}, u32[]{:S(2)}) collective-permute-start(bf16[144,1152]{1,0:T(8,128)(2,1)S(1)} %fusion.82), channel_id=1, source_target_pairs={{0,8},{8,16},{16,24},{24,28},{28,20},{20,12},{12,4},{4,0},{1,9},{9... | collective-permute-start | bytes 995336 | tf_op jit(solution)/shard_map/ppermute | solution.py:338
  577.1 13.1 %collective-permute-start.47 = (bf16[144,1152]{1,0:T(8,128)(2,1)S(1)}, bf16[144,1152]{1,0:T(8,128)(2,1)S(1)}, u32[]{:S(2)}, u32[]{:S(2)}) collective-permute-start(bf16[144,1152]{1,0:T(8,128)(2,1)S(1)} %fusion.75), channel_id=1, source_target_pairs={{0,8},{8,16},{16,24},{24,28},{28,20},{20,12},{12,4},{4,0},{1,9},{9... | collective-permute-start | bytes 995336 | tf_op jit(solution)/shard_map/ppermute | solution.py:338
  578.5 13.2 %collective-permute-start.14 = (bf16[144,1152]{1,0:T(8,128)(2,1)S(1)}, bf16[144,1152]{1,0:T(8,128)(2,1)S(1)}, u32[]{:S(2)}, u32[]{:S(2)}) collective-permute-start(bf16[144,1152]{1,0:T(8,128)(2,1)S(1)} %fusion.63), channel_id=1, source_target_pairs={{0,4},{8,0},{16,8},{24,16},{28,24},{20,28},{12,20},{4,12},{1,5},{9... | collective-permute-start | bytes 995336 | tf_op jit(solution)/shard_map/ppermute | solution.py:338
  584.3 13.1 %collective-permute-start.38 = (bf16[144,1152]{1,0:T(8,128)(2,1)S(1)}, bf16[144,1152]{1,0:T(8,128)(2,1)S(1)}, u32[]{:S(2)}, u32[]{:S(2)}) collective-permute-start(bf16[144,1152]{1,0:T(8,128)(2,1)S(1)} %fusion.81), channel_id=1, source_target_pairs={{0,8},{8,16},{16,24},{24,28},{28,20},{20,12},{12,4},{4,0},{1,9},{9... | collective-permute-start | bytes 995336 | tf_op jit(solution)/shard_map/ppermute | solution.py:338
  591.4 13.1 %collective-permute-start.48 = (bf16[144,1152]{1,0:T(8,128)(2,1)S(1)}, bf16[144,1152]{1,0:T(8,128)(2,1)S(1)}, u32[]{:S(2)}, u32[]{:S(2)}) collective-permute-start(bf16[144,1152]{1,0:T(8,128)(2,1)S(1)} %fusion.74), channel_id=1, source_target_pairs={{0,8},{8,16},{16,24},{24,28},{28,20},{20,12},{12,4},{4,0},{1,9},{9... | collective-permute-start | bytes 995336 | tf_op jit(solution)/shard_map/ppermute | solution.py:338
  592.8 13.2 %collective-permute-start.15 = (bf16[144,1152]{1,0:T(8,128)(2,1)S(1)}, bf16[144,1152]{1,0:T(8,128)(2,1)S(1)}, u32[]{:S(2)}, u32[]{:S(2)}) collective-permute-start(bf16[144,1152]{1,0:T(8,128)(2,1)S(1)} %fusion.62), channel_id=1, source_target_pairs={{0,2},{1,3},{2,0},{3,1},{4,6},{5,7},{6,4},{7,5},{8,10},{9,11},{10,... | collective-permute-start | bytes 995336 | tf_op jit(solution)/shard_map/ppermute | solution.py:389
  598.5 13.1 %collective-permute-start.39 = (bf16[144,1152]{1,0:T(8,128)(2,1)S(1)}, bf16[144,1152]{1,0:T(8,128)(2,1)S(1)}, u32[]{:S(2)}, u32[]{:S(2)}) collective-permute-start(bf16[144,1152]{1,0:T(8,128)(2,1)S(1)} %fusion.80), channel_id=1, source_target_pairs={{0,8},{8,16},{16,24},{24,28},{28,20},{20,12},{12,4},{4,0},{1,9},{9... | collective-permute-start | bytes 995336 | tf_op jit(solution)/shard_map/ppermute | solution.py:338
  605.6 13.1 %collective-permute-start.49 = (bf16[144,1152]{1,0:T(8,128)(2,1)S(1)}, bf16[144,1152]{1,0:T(8,128)(2,1)S(1)}, u32[]{:S(2)}, u32[]{:S(2)}) collective-permute-start(bf16[144,1152]{1,0:T(8,128)(2,1)S(1)} %fusion.73), channel_id=1, source_target_pairs={{0,8},{8,16},{16,24},{24,28},{28,20},{20,12},{12,4},{4,0},{1,9},{9... | collective-permute-start | bytes 995336 | tf_op jit(solution)/shard_map/ppermute | solution.py:338
  606.0 14.8 %collective-permute-start.16 = (bf16[144,1152]{1,0:T(8,128)(2,1)S(1)}, bf16[144,1152]{1,0:T(8,128)(2,1)S(1)}, u32[]{:S(2)}, u32[]{:S(2)}) collective-permute-start(bf16[144,1152]{1,0:T(8,128)(2,1)S(1)} %add_convert_fusion.5), channel_id=1, source_target_pairs={{0,1},{1,0},{2,3},{3,2},{4,5},{5,4},{6,7},{7,6},{8,9},{9,8},{10,11... | collective-permute-start | bytes 995336 | tf_op jit(solution)/shard_map/ppermute | solution.py:392
  613.4 13.3 %collective-permute-start.40 = (bf16[144,1152]{1,0:T(8,128)(2,1)}, bf16[144,1152]{1,0:T(8,128)(2,1)}, u32[]{:S(2)}, u32[]{:S(2)}) collective-permute-start(bf16[144,1152]{1,0:T(8,128)(2,1)} %fusion.79), channel_id=1, source_target_pairs={{0,8},{8,16},{16,24},{24,28},{28,20},{20,12},{12,4},{4,0},{1,9},{9... | collective-permute-start | bytes 995336 | tf_op jit(solution)/shard_map/ppermute | solution.py:338
  620.5 22.5 %collective-permute-start.50 = (bf16[144,1152]{1,0:T(8,128)(2,1)}, bf16[144,1152]{1,0:T(8,128)(2,1)}, u32[]{:S(2)}, u32[]{:S(2)}) collective-permute-start(bf16[144,1152]{1,0:T(8,128)(2,1)} %fusion.72), channel_id=1, source_target_pairs={{0,8},{8,16},{16,24},{24,28},{28,20},{20,12},{12,4},{4,0},{1,9},{9... | collective-permute-start | bytes 995336 | tf_op jit(solution)/shard_map/ppermute | solution.py:338
  625.2 10.8 %collective-permute-start.56 = (bf16[144,1152]{1,0:T(8,128)(2,1)S(1)}, bf16[144,1152]{1,0:T(8,128)(2,1)S(1)}, u32[]{:S(2)}, u32[]{:S(2)}) collective-permute-start(bf16[144,1152]{1,0:T(8,128)(2,1)S(1)} %get-tuple-element.101), channel_id=1, source_target_pairs={{0,4},{8,0},{16,8},{24,16},{28,24},{20,28},{12,20},{4,12},{1,5},{9... | collective-permute-start | bytes 995336 | tf_op jit(solution)/shard_map/ppermute | solution.py:338
  626.7 13.0 %collective-permute-start.63 = (bf16[144,1152]{1,0:T(8,128)(2,1)S(1)}, bf16[144,1152]{1,0:T(8,128)(2,1)S(1)}, u32[]{:S(2)}, u32[]{:S(2)}) collective-permute-start(bf16[144,1152]{1,0:T(8,128)(2,1)S(1)} %get-tuple-element.102), channel_id=1, source_target_pairs={{0,4},{8,0},{16,8},{24,16},{28,24},{20,28},{12,20},{4,12},{1,5},{9... | collective-permute-start | bytes 995336 | tf_op jit(solution)/shard_map/ppermute | solution.py:338
  628.0 30.4 %collective-permute-start.41 = (bf16[144,1152]{1,0:T(8,128)(2,1)S(1)}, bf16[144,1152]{1,0:T(8,128)(2,1)S(1)}, u32[]{:S(2)}, u32[]{:S(2)}) collective-permute-start(bf16[144,1152]{1,0:T(8,128)(2,1)S(1)} %fusion.78), channel_id=1, source_target_pairs={{0,8},{8,16},{16,24},{24,28},{28,20},{20,12},{12,4},{4,0},{1,9},{9... | collective-permute-start | bytes 995336 | tf_op jit(solution)/shard_map/ppermute | solution.py:338
  641.2 10.0 %collective-permute-start.57 = (bf16[144,1152]{1,0:T(8,128)(2,1)S(1)}, bf16[144,1152]{1,0:T(8,128)(2,1)S(1)}, u32[]{:S(2)}, u32[]{:S(2)}) collective-permute-start(bf16[144,1152]{1,0:T(8,128)(2,1)S(1)} %get-tuple-element.99), channel_id=1, source_target_pairs={{0,4},{8,0},{16,8},{24,16},{28,24},{20,28},{12,20},{4,12},{1,5},{9... | collective-permute-start | bytes 995336 | tf_op jit(solution)/shard_map/ppermute | solution.py:338
  642.4 12.3 %collective-permute-start.64 = (bf16[144,1152]{1,0:T(8,128)(2,1)S(1)}, bf16[144,1152]{1,0:T(8,128)(2,1)S(1)}, u32[]{:S(2)}, u32[]{:S(2)}) collective-permute-start(bf16[144,1152]{1,0:T(8,128)(2,1)S(1)} %get-tuple-element.100), channel_id=1, source_target_pairs={{0,4},{8,0},{16,8},{24,16},{28,24},{20,28},{12,20},{4,12},{1,5},{9... | collective-permute-start | bytes 995336 | tf_op jit(solution)/shard_map/ppermute | solution.py:338
  644.3 29.2 %collective-permute-start.51 = (bf16[144,1152]{1,0:T(8,128)(2,1)S(1)}, bf16[144,1152]{1,0:T(8,128)(2,1)S(1)}, u32[]{:S(2)}, u32[]{:S(2)}) collective-permute-start(bf16[144,1152]{1,0:T(8,128)(2,1)S(1)} %fusion.71), channel_id=1, source_target_pairs={{0,8},{8,16},{16,24},{24,28},{28,20},{20,12},{12,4},{4,0},{1,9},{9... | collective-permute-start | bytes 995336 | tf_op jit(solution)/shard_map/ppermute | solution.py:338
  657.4 12.3 %collective-permute-start.65 = (bf16[144,1152]{1,0:T(8,128)(2,1)S(1)}, bf16[144,1152]{1,0:T(8,128)(2,1)S(1)}, u32[]{:S(2)}, u32[]{:S(2)}) collective-permute-start(bf16[144,1152]{1,0:T(8,128)(2,1)S(1)} %get-tuple-element.98), channel_id=1, source_target_pairs={{0,4},{8,0},{16,8},{24,16},{28,24},{20,28},{12,20},{4,12},{1,5},{9... | collective-permute-start | bytes 995336 | tf_op jit(solution)/shard_map/ppermute | solution.py:338
  659.6 28.9 %collective-permute-start.42 = (bf16[144,1152]{1,0:T(8,128)(2,1)S(1)}, bf16[144,1152]{1,0:T(8,128)(2,1)S(1)}, u32[]{:S(2)}, u32[]{:S(2)}) collective-permute-start(bf16[144,1152]{1,0:T(8,128)(2,1)S(1)} %fusion.77), channel_id=1, source_target_pairs={{0,8},{8,16},{16,24},{24,28},{28,20},{20,12},{12,4},{4,0},{1,9},{9... | collective-permute-start | bytes 995336 | tf_op jit(solution)/shard_map/ppermute | solution.py:338
  672.5 12.4 %collective-permute-start.66 = (bf16[144,1152]{1,0:T(8,128)(2,1)S(1)}, bf16[144,1152]{1,0:T(8,128)(2,1)S(1)}, u32[]{:S(2)}, u32[]{:S(2)}) collective-permute-start(bf16[144,1152]{1,0:T(8,128)(2,1)S(1)} %get-tuple-element.96), channel_id=1, source_target_pairs={{0,4},{8,0},{16,8},{24,16},{28,24},{20,28},{12,20},{4,12},{1,5},{9... | collective-permute-start | bytes 995336 | tf_op jit(solution)/shard_map/ppermute | solution.py:338
  674.7 29.2 %collective-permute-start.52 = (bf16[144,1152]{1,0:T(8,128)(2,1)S(1)}, bf16[144,1152]{1,0:T(8,128)(2,1)S(1)}, u32[]{:S(2)}, u32[]{:S(2)}) collective-permute-start(bf16[144,1152]{1,0:T(8,128)(2,1)S(1)} %fusion.70), channel_id=1, source_target_pairs={{0,8},{8,16},{16,24},{24,28},{28,20},{20,12},{12,4},{4,0},{1,9},{9... | collective-permute-start | bytes 995336 | tf_op jit(solution)/shard_map/ppermute | solution.py:338
  687.6 12.3 %collective-permute-start.67 = (bf16[144,1152]{1,0:T(8,128)(2,1)S(1)}, bf16[144,1152]{1,0:T(8,128)(2,1)S(1)}, u32[]{:S(2)}, u32[]{:S(2)}) collective-permute-start(bf16[144,1152]{1,0:T(8,128)(2,1)S(1)} %get-tuple-element.94), channel_id=1, source_target_pairs={{0,4},{8,0},{16,8},{24,16},{28,24},{20,28},{12,20},{4,12},{1,5},{9... | collective-permute-start | bytes 995336 | tf_op jit(solution)/shard_map/ppermute | solution.py:338
  689.8 29.6 %collective-permute-start.43 = (bf16[144,1152]{1,0:T(8,128)(2,1)S(1)}, bf16[144,1152]{1,0:T(8,128)(2,1)S(1)}, u32[]{:S(2)}, u32[]{:S(2)}) collective-permute-start(bf16[144,1152]{1,0:T(8,128)(2,1)S(1)} %fusion.76), channel_id=1, source_target_pairs={{0,2},{1,3},{2,0},{3,1},{4,6},{5,7},{6,4},{7,5},{8,10},{9,11},{10,... | collective-permute-start | bytes 995336 | tf_op jit(solution)/shard_map/ppermute | solution.py:389
  702.9 12.9 %collective-permute-start.68 = (bf16[144,1152]{1,0:T(8,128)(2,1)S(1)}, bf16[144,1152]{1,0:T(8,128)(2,1)S(1)}, u32[]{:S(2)}, u32[]{:S(2)}) collective-permute-start(bf16[144,1152]{1,0:T(8,128)(2,1)S(1)} %get-tuple-element.92), channel_id=1, source_target_pairs={{0,4},{8,0},{16,8},{24,16},{28,24},{20,28},{12,20},{4,12},{1,5},{9... | collective-permute-start | bytes 995336 | tf_op jit(solution)/shard_map/ppermute | solution.py:338
  705.1 24.9 %collective-permute-start.53 = (bf16[144,1152]{1,0:T(8,128)(2,1)S(1)}, bf16[144,1152]{1,0:T(8,128)(2,1)S(1)}, u32[]{:S(2)}, u32[]{:S(2)}) collective-permute-start(bf16[144,1152]{1,0:T(8,128)(2,1)S(1)} %fusion.69), channel_id=1, source_target_pairs={{0,2},{1,3},{2,0},{3,1},{4,6},{5,7},{6,4},{7,5},{8,10},{9,11},{10,... | collective-permute-start | bytes 995336 | tf_op jit(solution)/shard_map/ppermute | solution.py:389
  719.5 10.6 %collective-permute-start.44 = (bf16[144,1152]{1,0:T(8,128)(2,1)S(1)}, bf16[144,1152]{1,0:T(8,128)(2,1)S(1)}, u32[]{:S(2)}, u32[]{:S(2)}) collective-permute-start(bf16[144,1152]{1,0:T(8,128)(2,1)S(1)} %add_convert_fusion.3), channel_id=1, source_target_pairs={{0,1},{1,0},{2,3},{3,2},{4,5},{5,4},{6,7},{7,6},{8,9},{9,8},{10,11... | collective-permute-start | bytes 995336 | tf_op jit(solution)/shard_map/ppermute | solution.py:392
  729.7 10.7 %collective-permute-start.70 = (bf16[288,1152]{1,0:T(8,128)(2,1)S(1)}, bf16[288,1152]{1,0:T(8,128)(2,1)S(1)}, u32[]{:S(2)}, u32[]{:S(2)}) collective-permute-start(bf16[288,1152]{1,0:T(8,128)(2,1)S(1)} %pad_maximum_fusion.13), channel_id=1, source_target_pairs={{0,2},{1,3},{2,0},{3,1},{4,6},{5,7},{6,4},{7,5},{8,10},{9,11},{10,... | collective-permute-start | bytes 1990664 | tf_op jit(solution)/shard_map/ppermute | solution.py:389
  730.0 10.6 %collective-permute-start.54 = (bf16[144,1152]{1,0:T(8,128)(2,1)S(1)}, bf16[144,1152]{1,0:T(8,128)(2,1)S(1)}, u32[]{:S(2)}, u32[]{:S(2)}) collective-permute-start(bf16[144,1152]{1,0:T(8,128)(2,1)S(1)} %add_convert_fusion.1), channel_id=1, source_target_pairs={{0,1},{1,0},{2,3},{3,2},{4,5},{5,4},{6,7},{7,6},{8,9},{9,8},{10,11... | collective-permute-start | bytes 995336 | tf_op jit(solution)/shard_map/ppermute | solution.py:392
  (72 other events, 735.9 us)
